TPU v7x, 1024 devices: a whole 4x8x16 slice. The times are simulated.
1024 devices in a mesh: expert: 64 (over z, x), cuts: 2 (over core), dp: 8 (over y).
Axes of the slice: x: 4, y: 8, z: 16, core: 2. Of those that a mesh axis runs over, the one named last changes fastest.
Arguments:
- tokens: bfloat16 [12288, 2048], P(('expert', 'dp')), may hold values from -6 to 6
- out_grad: bfloat16 [12288, 2048], P(('expert', 'dp')), may hold values from -6 to 6
- expert_ids: int32 [12288, 8], P(('expert', 'dp')), may hold values from 0 to 63, all different within a row; in each aligned block of 24 rows (0 to 23, 24 to 47, ...) at most 4 rows name the same one
- route_probs: float32 [12288, 8], P(('expert', 'dp')), may hold values from 0.05 to 0.6
- gate_weight: bfloat16 [2048, 64, 768], P(None, 'expert', 'cuts'), may hold values from -0.125 to 0.125
- up_weight: bfloat16 [2048, 64, 768], P(None, 'expert', 'cuts'), may hold values from -0.125 to 0.125
- down_weight: bfloat16 [768, 64, 2048], P('cuts', 'expert'), may hold values from -0.21875 to 0.21875
Outputs:
- token_grad: bfloat16 [12288, 2048], P(('expert', 'dp'), 'cuts')
- gate_grad: bfloat16 [2048, 64, 768], P('dp', 'expert', 'cuts')
- up_grad: bfloat16 [2048, 64, 768], P('dp', 'expert', 'cuts')
- down_grad: bfloat16 [768, 64, 2048], P(('cuts', 'dp'), 'expert')
Inputs may be any that keep to these rules, and one draw needn't show every extreme that they name: `expert_ids`: each row names 8 different experts. In each aligned block of 24 rows (the tokens of one device) no expert is named by more than 4 rows, a bound that some block reaches.
All inputs are finite; a program needn't handle non-finite values.
Results may differ from a plain program's by a relative error of at most 0.017.
Values may be sent and summed in bfloat16 or wider, within the bound.
No kernel may reach another device: no remote copies, remote signals or barrier semaphores. Data moves between devices by JAX's collectives and lax.ppermute only.
A program may use at most 64 MiB of HBM per device.

v0:
```python
import jax
import jax.numpy as jnp
from jax import lax
from jax.sharding import PartitionSpec as P

EXPERTS = 64
CAP = 4


def shards(tokens, out_grad, expert_ids, route_probs, gate_weight, up_weight, down_weight):
    tok_rows, width = tokens.shape
    top_count = expert_ids.shape[1]
    sources = lax.axis_size("expert")
    local_experts = gate_weight.shape[1]
    slots = EXPERTS * CAP
    routing = expert_ids.reshape(-1)
    onehot = (routing[:, None] == jnp.arange(EXPERTS, dtype=jnp.int32)[None, :]).astype(jnp.int32)
    earlier = jnp.cumsum(onehot, axis=0) - onehot
    slot_of = routing * CAP + jnp.sum(earlier * onehot, axis=1)
    placing = (slot_of[None, :] == jnp.arange(slots, dtype=jnp.int32)[:, None]).reshape(
        slots, tok_rows, top_count
    )
    picked = jnp.sum(placing.astype(jnp.float32), axis=2)
    weighed = jnp.sum(jnp.where(placing, route_probs[None, :, :], 0.0), axis=2)
    send_rows = jnp.dot(
        picked.astype(jnp.bfloat16), tokens, preferred_element_type=jnp.float32
    ).astype(jnp.bfloat16)
    send_grads = jnp.dot(
        weighed, out_grad.astype(jnp.float32), precision=lax.Precision.HIGHEST
    ).astype(jnp.bfloat16)
    got_rows, got_grads = (
        lax.all_to_all(send_rows, "expert", split_axis=0, concat_axis=0, tiled=True),
        lax.all_to_all(send_grads, "expert", split_axis=0, concat_axis=0, tiled=True),
    )
    layout = (sources, local_experts, CAP, width)
    rows_in = got_rows.reshape(layout)
    rows_grad = got_grads.reshape(layout)
    gate_val = jnp.einsum(
        "secd,def->secf", rows_in, gate_weight, preferred_element_type=jnp.float32
    )
    up_val = jnp.einsum("secd,def->secf", rows_in, up_weight, preferred_element_type=jnp.float32)
    sigma = jax.nn.sigmoid(gate_val)
    activated = gate_val * sigma
    slope = sigma * (1.0 + gate_val * (1.0 - sigma))
    hidden = (activated * up_val).astype(jnp.bfloat16)
    back_hid = jnp.einsum(
        "secd,fed->secf", rows_grad, down_weight, preferred_element_type=jnp.float32
    )
    gate_back = (back_hid * up_val * slope).astype(jnp.bfloat16)
    up_back = (back_hid * activated).astype(jnp.bfloat16)
    stacked = jnp.stack((gate_back, up_back), axis=3)
    piece = rows_in
    proj_sum = lax.psum_scatter(
        jnp.einsum("secd,secgf->degf", piece, stacked, preferred_element_type=jnp.float32).astype(
            jnp.bfloat16
        ),
        "dp",
        scatter_dimension=0,
        tiled=True,
    ).astype(jnp.float32)
    piece = hidden
    down_sum = lax.psum_scatter(
        jnp.einsum("secf,secd->fed", piece, rows_grad, preferred_element_type=jnp.float32).astype(
            jnp.bfloat16
        ),
        "dp",
        scatter_dimension=0,
        tiled=True,
    )
    row_grads = jnp.einsum(
        "secf,def->secd", gate_back, gate_weight, preferred_element_type=jnp.float32
    )
    row_grads = row_grads + jnp.einsum(
        "secf,def->secd", up_back, up_weight, preferred_element_type=jnp.float32
    )
    row_grads = row_grads.reshape(slots, width)
    returned = lax.all_to_all(
        row_grads.astype(jnp.bfloat16), "expert", split_axis=0, concat_axis=0, tiled=True
    ).astype(row_grads.dtype)
    combined = jnp.dot(picked.T, returned, precision=lax.Precision.HIGHEST)
    result = lax.psum_scatter(
        combined.astype(jnp.bfloat16), "cuts", scatter_dimension=1, tiled=True
    )
    gate_grad = proj_sum[:, :, 0, :].astype(jnp.bfloat16)
    up_grad = proj_sum[:, :, 1, :].astype(jnp.bfloat16)
    return (result, gate_grad, up_grad, down_sum)


def solution(mesh):
    placed = (
        P(("expert", "dp"), None),
        P(("expert", "dp"), None),
        P(("expert", "dp"), None),
        P(("expert", "dp"), None),
        P(None, "expert", "cuts"),
        P(None, "expert", "cuts"),
        P("cuts", "expert", None),
    )
    return jax.shard_map(
        shards,
        mesh=mesh,
        in_specs=placed,
        out_specs=(
            P(("expert", "dp"), "cuts"),
            P("dp", "expert", "cuts"),
            P("dp", "expert", "cuts"),
            P(("cuts", "dp"), "expert", None),
        ),
        check_vma=False,
    )
```

profile of v0, /device:TPU:1, one launch (start us, length us, event | category | flops | bytes accessed | tf_op | source)
XLA Modules:
  0.0 354.6 jit_solution(13346368254071461539)
XLA Ops:
  7.2 0.9 copy.44
  9.3 0.8 copy.48
  10.2 1.3 convolution_convert_fusion
  11.6 1.2 all_to_all.20
  12.8 23.2 %all-to-all-start.1 = ((bf16[64,4,2048]{2,1,0:T(4,128)(2,1)}), bf16[64,4,2048]{2,1,0:T(4,128)(2,1)}, u32[]{:S(2)}, u32[]{:S(2)}) async-start(bf16[64,4,2048]{2,1,0:T(4,128)(2,1)} %all_to_all.20), calls=%async_computation.1 | async-start | bytes 2097152 | tf_op jit(solution)/shard_map/all_to_all | solution.py:32
  36.0 1.0 convolution_convert_fusion.1
  37.0 1.2 all_to_all.18
  38.3 49.0 %all-to-all-done.1 = bf16[64,4,2048]{2,1,0:T(4,128)(2,1)} async-done(((bf16[64,4,2048]{2,1,0:T(4,128)(2,1)}), bf16[64,4,2048]{2,1,0:T(4,128)(2,1)}, u32[]{:S(2)}, u32[]{:S(2)}) %all-to-all-start.1) | async-done | bytes 1048608 | tf_op jit(solution)/shard_map/all_to_all | solution.py:32
  87.3 9.3 %all-to-all-start = ((bf16[64,4,2048]{2,1,0:T(4,128)(2,1)}), bf16[64,4,2048]{2,1,0:T(4,128)(2,1)}, u32[]{:S(2)}, u32[]{:S(2)}) async-start(bf16[64,4,2048]{2,1,0:T(4,128)(2,1)} %all_to_all.18), calls=%async_computation | async-start | bytes 2097152 | tf_op jit(solution)/shard_map/all_to_all | solution.py:33
  96.6 3.0 fusion.15
  99.6 2.9 fusion.18
  102.5 44.9 %all-to-all-done = bf16[64,4,2048]{2,1,0:T(4,128)(2,1)} async-done(((bf16[64,4,2048]{2,1,0:T(4,128)(2,1)}), bf16[64,4,2048]{2,1,0:T(4,128)(2,1)}, u32[]{:S(2)}, u32[]{:S(2)}) %all-to-all-start) | async-done | bytes 1048608 | tf_op jit(solution)/shard_map/all_to_all | solution.py:33
  147.4 3.6 %fusion.1 = bf16[384,1,2048]{0,2,1:T(8,128)(2,1)} fusion(bf16[64,4,2048]{2,1,0:T(4,128)(2,1)} %all-to-all-done, f32[64,1,4,384]{3,0,2,1:T(8,128)} %fusion.15, f32[64,1,4,384]{3,0,2,1:T(8,128)} %fusion.18), kind=kOutput, calls=%fused_computation.4 | convolution fusion | flops 404029440 | bytes 3407872 | tf_op jit(solution)/shard_map/secf,secd->fed/dot_general | solution.py:63
  151.0 8.5 %copy.55 = bf16[384,1,2048]{2,1,0:T(2,128)(2,1)} copy(bf16[384,1,2048]{0,2,1:T(8,128)(2,1)} %fusion.1) | data formatting | bytes 3145728 | tf_op jit(solution)/shard_map/convert_element_type | solution.py:63
  159.6 2.9 multiply_convert_fusion.1
  162.5 0.7 copy-done.2
  163.2 4.7 %fusion = bf16[2048,1,2,384]{0,3,2,1:T(8,128)(2,1)} fusion(bf16[64,4,2048]{2,1,0:T(4,128)(2,1)} %all-to-all-done.1, bf16[64,1,4,1,384]{4,0,2,3,1:T(8,128)(2,1)S(1)} %bitcast.98, bf16[64,1,4,1,384]{4,0,2,3,1:T(8,128)(2,1)S(1)} %bitcast.99), kind=kOutput, calls=%fused_computation.2 | convolution fusion | flops 807075840 | bytes 4587520 | tf_op jit(solution)/shard_map/secd,secgf->degf/dot_general | solution.py:54
  167.9 1.7 fusion.3
  169.5 0.8 fusion.2
  170.3 1.8 copy.52
  172.1 8.8 %all-to-all-start.2 = ((bf16[64,4,2048]{2,1,0:T(4,128)(2,1)}), bf16[64,4,2048]{2,1,0:T(4,128)(2,1)S(1)}, u32[]{:S(2)}, u32[]{:S(2)}) async-start(bf16[64,4,2048]{2,1,0:T(4,128)(2,1)} %copy.52), calls=%async_computation.2 | async-start | bytes 2097152 | tf_op jit(solution)/shard_map/all_to_all | solution.py:77
  180.9 1.3 dynamic-slice
  182.8 79.4 %all-reduce.4.cloned.1.call-done = bf16[384,1,2048]{2,1,0:T(2,128)(2,1)} async-done(((bf16[384,1,2048]{2,1,0:T(2,128)(2,1)}), bf16[384,1,2048]{2,1,0:T(2,128)(2,1)}) %all-reduce.4.cloned.1.call-update) | async-done | bytes 1572880
  262.3 1.4 constant_dynamic-slice_fusion
  263.7 0.8 copy.58
  264.5 1.1 all_to_all.23
  265.6 2.4 convolution_convert_fusion.2
  268.0 50.0 %reduce-scatter.5.cloned.1.call-done = bf16[256,1,2,384]{0,3,2,1:T(8,128)(2,1)} async-done(((bf16[2048,1,2,384]{0,3,2,1:T(8,128)(2,1)}), bf16[256,1,2,384]{0,3,2,1:T(8,128)(2,1)}) %reduce-scatter.5.cloned.1.call-update) | async-done | bytes 393232 | tf_op jit(solution)/shard_map/reduce_scatter | solution.py:53
  318.0 1.0 slice_bitcast_fusion
  319.0 0.8 copy.56
  319.9 0.8 copy.57
  320.7 27.4 %reduce-scatter.3.cloned.1.call-done = bf16[24,1024]{1,0:T(8,128)(2,1)} async-done(((bf16[24,2048]{1,0:T(8,128)(2,1)}), bf16[24,1024]{1,0:T(8,128)(2,1)}) %reduce-scatter.3.cloned.1.call-update) | async-done | bytes 49168 | tf_op jit(solution)/shard_map/reduce_scatter | solution.py:81
  (26 shorter events, 1.5 us)
Async XLA Ops:
  7.2 92.4 %copy-start = (bf16[2048,1,384]{2,0,1:T(8,128)(2,1)S(1)}, bf16[2048,1,384]{2,0,1:T(8,128)(2,1)}, u32[]{:S(2)}) copy-start(bf16[2048,1,384]{2,0,1:T(8,128)(2,1)} %param.11) | copy-start | bytes 4718596
  12.8 23.2 %copy-start.3 = (bf16[24,2048]{1,0:T(8,128)(2,1)S(1)}, bf16[24,2048]{1,0:T(8,128)(2,1)}, u32[]{:S(2)}) copy-start(bf16[24,2048]{1,0:T(8,128)(2,1)} %param.8) | copy-start | bytes 294916
  12.8 74.5 %all-to-all-start.1 = ((bf16[64,4,2048]{2,1,0:T(4,128)(2,1)}), bf16[64,4,2048]{2,1,0:T(4,128)(2,1)}, u32[]{:S(2)}, u32[]{:S(2)}) async-start(bf16[64,4,2048]{2,1,0:T(4,128)(2,1)} %all_to_all.20), calls=%async_computation.1 | async-start | bytes 2097152 | tf_op jit(solution)/shard_map/all_to_all | solution.py:32
  38.3 58.4 %copy-start.1 = (bf16[2048,1,384]{2,0,1:T(8,128)(2,1)S(1)}, bf16[2048,1,384]{2,0,1:T(8,128)(2,1)}, u32[]{:S(2)}) copy-start(bf16[2048,1,384]{2,0,1:T(8,128)(2,1)} %param.12) | copy-start | bytes 4718596
  87.3 60.1 %all-to-all-start = ((bf16[64,4,2048]{2,1,0:T(4,128)(2,1)}), bf16[64,4,2048]{2,1,0:T(4,128)(2,1)}, u32[]{:S(2)}, u32[]{:S(2)}) async-start(bf16[64,4,2048]{2,1,0:T(4,128)(2,1)} %all_to_all.18), calls=%async_computation | async-start | bytes 2097152 | tf_op jit(solution)/shard_map/all_to_all | solution.py:33
  96.6 165.7 %all-reduce.4.cloned.1.call-start = ((), (), s32[]{:S(2)}) async-start(), calls=%async_computation.7 | async-start | bytes 6291456
  159.5 158.5 %reduce-scatter.5.cloned.1.call-start = ((), (), s32[]{:S(2)}) async-start(), calls=%async_computation.6 | async-start | bytes 3538944 | tf_op jit(solution)/shard_map/reduce_scatter | solution.py:53
  162.5 0.7 copy-start.2
  172.1 92.4 %all-to-all-start.2 = ((bf16[64,4,2048]{2,1,0:T(4,128)(2,1)}), bf16[64,4,2048]{2,1,0:T(4,128)(2,1)S(1)}, u32[]{:S(2)}, u32[]{:S(2)}) async-start(bf16[64,4,2048]{2,1,0:T(4,128)(2,1)} %copy.52), calls=%async_computation.2 | async-start | bytes 2097152 | tf_op jit(solution)/shard_map/all_to_all | solution.py:77
  180.9 167.2 %reduce-scatter.3.cloned.1.call-start = ((), (), s32[]{:S(2)}) async-start(), calls=%async_computation.5 | async-start | bytes 147456 | tf_op jit(solution)/shard_map/reduce_scatter | solution.py:81
Sparse Core Ops, SparseCore 0:
  159.6 102.6 all-reduce.3
  265.7 52.2 reduce-scatter.4
  321.9 26.1 reduce-scatter.2
where the time goes:
time: 356 us; the launch traced here: 355 us
  waiting for transfers between devices  251 us (71%)
  starting transfers between devices  41.3 us (12%)
  matrix products  24.3 us (7%)
  local copies, waits for them, and re-layouts  22.7 us (6%)
  between operations  14.6 us (4%)
    unnamed x4, waiting for transfers between devices  79.5 us
    reduce_scatter x1, waiting for transfers between devices, shards(): lax.psum_scatter(jnp.einsum('secd,secgf->degf', piece, stacked, preferred...  50 us
    all_to_all x1, waiting for transfers between devices, shards(): lax.all_to_all(send_rows, 'expert', split_axis=0, concat_axis=0, tiled=True)  49 us
    all_to_all x1, waiting for transfers between devices, shards(): lax.all_to_all(send_grads, 'expert', split_axis=0, concat_axis=0, tiled=T...  44.9 us
    reduce_scatter x1, waiting for transfers between devices, shards(): lax.psum_scatter(combined.astype(jnp.bfloat16), 'cuts', scatter_dimension...  27.4 us
    all_to_all x1, starting transfers between devices, shards(): lax.all_to_all(send_rows, 'expert', split_axis=0, concat_axis=0, tiled=True)  23.2 us
    all_to_all x1, starting transfers between devices, shards(): lax.all_to_all(send_grads, 'expert', split_axis=0, concat_axis=0, tiled=T...  9.29 us
    all_to_all x1, starting transfers between devices, shards(): lax.all_to_all(row_grads.astype(jnp.bfloat16), 'expert', split_axis=0, co...  8.76 us
  transfers between devices with their start and end apart: 6, of which 5 were waited for; matrix products, arithmetic and copies ran while one was open for 8% of the time, Pallas kernels for 0%

commit v1 on v0

v1 whole, which is shorter than its diff:
```python
import jax
import jax.numpy as jnp
from jax import lax
from jax.sharding import PartitionSpec as P

EXPERTS = 64
CAP = 4


def shards(tokens, out_grad, expert_ids, route_probs, gate_weight, up_weight, down_weight):
    rows, width = tokens.shape
    top = expert_ids.shape[1]
    half = width // 2
    hidden_dim = gate_weight.shape[2]
    slots = EXPERTS * CAP
    replicas = lax.axis_size("dp")
    cut = lax.axis_index("cuts")
    first = cut == 0
    swap = [(0, 1), (1, 0)]

    named = (
        expert_ids[:, :, None] == jnp.arange(EXPERTS, dtype=jnp.int32)[None, None, :]
    )
    names = jnp.sum(named.astype(jnp.float32), axis=1)
    before = jnp.arange(rows)[:, None] > jnp.arange(rows)[None, :]
    rank = jnp.dot(
        before.astype(jnp.bfloat16), names.astype(jnp.bfloat16), preferred_element_type=jnp.float32
    )
    prob = jnp.sum(jnp.where(named, route_probs[:, :, None], 0.0), axis=1)
    place = jnp.where(names > 0, rank, -1.0)
    slot_rank = jnp.arange(slots) % CAP
    place_t = jnp.repeat(place.T, CAP, axis=0)
    prob_t = jnp.repeat(prob.T, CAP, axis=0)
    hit = place_t == slot_rank[:, None].astype(jnp.float32)
    picked = jnp.where(hit, 1.0, 0.0).astype(jnp.bfloat16)
    weighed = jnp.where(hit, prob_t, 0.0)
    factor = jnp.where(first, picked.astype(jnp.float32), weighed)
    high = lax.reduce_precision(factor, 8, 7)
    middle = lax.reduce_precision(factor - high, 8, 7)
    low = factor - high - middle
    factors = jnp.concatenate((high, middle, low), axis=1).astype(jnp.bfloat16)
    source = jnp.where(first, tokens, out_grad)
    sent = jnp.dot(
        factors, jnp.concatenate((source,) * 3, axis=0), preferred_element_type=jnp.float32
    ).astype(jnp.bfloat16)
    own = lax.all_to_all(
        sent.reshape(EXPERTS, CAP, width), "expert", split_axis=0, concat_axis=0, tiled=True
    ).reshape(slots, width)
    peer = lax.ppermute(own, "cuts", swap)
    rows_in = jnp.where(first, own, peer)
    rows_grad = jnp.where(first, peer, own)

    w_gate = gate_weight[:, 0, :]
    w_up = up_weight[:, 0, :]
    w_down = down_weight[:, 0, :]

    def dot(a, b, da, db):
        return lax.dot_general(a, b, (((da,), (db,)), ((), ())), preferred_element_type=jnp.float32)

    gate_val = dot(rows_in, w_gate, 1, 0)
    up_val = dot(rows_in, w_up, 1, 0)
    sigma = jax.nn.sigmoid(gate_val)
    activated = gate_val * sigma
    slope = sigma * (1.0 + gate_val * (1.0 - sigma))
    hidden = (activated * up_val).astype(jnp.bfloat16)
    back_hid = dot(rows_grad, w_down, 1, 1)
    gate_back = (back_hid * up_val * slope).astype(jnp.bfloat16)
    up_back = (back_hid * activated).astype(jnp.bfloat16)

    tiles = hidden_dim // 128
    share = width // replicas
    strip = hidden_dim // replicas

    def packed(grad):
        return grad.reshape(replicas, share, tiles, 128).transpose(0, 2, 1, 3)

    down = dot(hidden, rows_grad, 0, 0).astype(jnp.bfloat16)
    down = down.reshape(replicas, strip, width // 128, 128).transpose(0, 2, 1, 3)
    parts = [
        packed(dot(rows_in, gate_back, 0, 0).astype(jnp.bfloat16)),
        packed(dot(rows_in, up_back, 0, 0).astype(jnp.bfloat16)),
        down,
    ]
    flat = jnp.concatenate([part.reshape(replicas, tiles * share, 128) for part in parts], axis=1)
    total = lax.psum_scatter(flat, "dp", scatter_dimension=0, tiled=True)[0]

    row_grads = dot(gate_back, w_gate, 1, 1) + dot(up_back, w_up, 1, 1)
    mine = jnp.where(first, row_grads[:, :half], row_grads[:, half:])
    other = jnp.where(first, row_grads[:, half:], row_grads[:, :half])
    mine = mine + lax.ppermute(other.astype(jnp.bfloat16), "cuts", swap).astype(jnp.float32)
    returned = lax.all_to_all(
        mine.astype(jnp.bfloat16).reshape(EXPERTS, CAP, half),
        "expert", split_axis=0, concat_axis=0, tiled=True,
    ).reshape(slots, half)
    result = dot(picked, returned, 0, 0).astype(jnp.bfloat16)

    size = tiles * share

    def unpacked(block):
        return block.reshape(tiles, share, 128).transpose(1, 0, 2).reshape(share, 1, hidden_dim)

    down_grad = (
        total[2 * size :].reshape(width // 128, strip, 128).transpose(1, 0, 2)
        .reshape(strip, 1, width)
    )
    return (result, unpacked(total[:size]), unpacked(total[size : 2 * size]), down_grad)


def solution(mesh):
    placed = (
        P(("expert", "dp"), None),
        P(("expert", "dp"), None),
        P(("expert", "dp"), None),
        P(("expert", "dp"), None),
        P(None, "expert", "cuts"),
        P(None, "expert", "cuts"),
        P("cuts", "expert", None),
    )
    return jax.shard_map(
        shards,
        mesh=mesh,
        in_specs=placed,
        out_specs=(
            P(("expert", "dp"), "cuts"),
            P("dp", "expert", "cuts"),
            P("dp", "expert", "cuts"),
            P(("cuts", "dp"), "expert", None),
        ),
        check_vma=False,
    )
```

time: 356 us -> 197 us (0.55)
  waiting for transfers between devices: 251 us -> 49.1 us
  blocking collectives: 0 us -> 74.3 us
  starting transfers between devices: 41.3 us -> 15.8 us
  matrix products: 24.3 us -> 9.66 us
  local copies, waits for them, and re-layouts: 22.7 us -> 28.2 us
  other arithmetic: 0.99 us -> 5.23 us
    unnamed x4 -> x1, waiting for transfers between devices: 79.5 us -> 0.02 us
    all_to_all x0 -> x1, blocking collectives: none -> 74.3 us  [shards(): lax.all_to_all(sent.reshape(EXPERTS, CAP, width), 'expert', split_axis=0,...]
    reduce_scatter x2 -> x1, waiting for transfers between devices: 77.4 us -> 14.4 us  [shards(): total = lax.psum_scatter(flat, 'dp', scatter_dimension=0, tiled=True)[0]]
    all_to_all x3 -> x1, waiting for transfers between devices: 93.9 us -> 31 us  [shards(): lax.all_to_all(mine.astype(jnp.bfloat16).reshape(EXPERTS, CAP, half), 'ex...]
    all_to_all x3 -> x1, starting transfers between devices: 41.2 us -> 5.55 us  [shards(): lax.all_to_all(mine.astype(jnp.bfloat16).reshape(EXPERTS, CAP, half), 'ex...]
    dot_general x10 -> x11, matrix products: 24.3 us -> 9.66 us  [the longest x9 9.07 us: dot(): lax.dot_general(a, b, (((da,), (db,)), ((), ())), preferred_element_type=...]
    ppermute x0 -> x2, starting transfers between devices: none -> 10.2 us  [the longest x1 6.72 us: shards(): peer = lax.ppermute(own, 'cuts', swap)]
    convert_element_type x3 -> x2, local copies, waits for them, and re-layouts: 11.3 us -> 4.31 us  [the longest x1 2.61 us: shards(): dot(rows_in, up_back, 0, 0).astype(jnp.bfloat16)]
  transfers between devices with their start and end apart: 6 -> 4, of which waited for: 5 -> 4; matrix products, arithmetic and copies ran while one was open for 8% -> 2% of each run, Pallas kernels for 0% -> 0%
where the time goes in v1:
time: 197 us
  blocking collectives  74.3 us (38%)
  waiting for transfers between devices  49.1 us (25%)
  local copies, waits for them, and re-layouts  28.2 us (14%)
  starting transfers between devices  15.8 us (8%)
  between operations  14.3 us (7%)
  matrix products  9.66 us (5%)
  other arithmetic  5.23 us (3%)
    all_to_all x1, blocking collectives, shards(): lax.all_to_all(sent.reshape(EXPERTS, CAP, width), 'expert', split_axis=0,...  74.3 us
    all_to_all x1, waiting for transfers between devices, shards(): lax.all_to_all(mine.astype(jnp.bfloat16).reshape(EXPERTS, CAP, half), 'ex...  31 us
    reduce_scatter x1, waiting for transfers between devices, shards(): total = lax.psum_scatter(flat, 'dp', scatter_dimension=0, tiled=True)[0]  14.4 us
    unnamed x22, local copies, waits for them, and re-layouts  10.4 us
    dot_general x9, matrix products, dot(): lax.dot_general(a, b, (((da,), (db,)), ((), ())), preferred_element_type=...  9.07 us
    ppermute x1, starting transfers between devices, shards(): peer = lax.ppermute(own, 'cuts', swap)  6.72 us
    transpose x2, local copies, waits for them, and re-layouts, packed(): return grad.reshape(replicas, share, tiles, 128).transpose(0, 2, 1, 3)  5.89 us
    all_to_all x1, starting transfers between devices, shards(): lax.all_to_all(mine.astype(jnp.bfloat16).reshape(EXPERTS, CAP, half), 'ex...  5.55 us
  transfers between devices with their start and end apart: 4, of which 4 were waited for; matrix products, arithmetic and copies ran while one was open for 2% of the time, Pallas kernels for 0%

profile of v1, /device:TPU:1, one launch (start us, length us, event | category | flops | bytes accessed | tf_op | source)
XLA Modules:
  0.0 196.6 jit_solution(8032218065289694222)
XLA Ops:
  7.2 0.9 copy.89
  8.1 0.8 copy.92
  9.5 0.9 broadcast_select_fusion.4
  10.9 1.2 reshape.88
  12.1 74.3 %all_to_all.10 = bf16[64,4,2048]{2,1,0:T(4,128)(2,1)} all-to-all(bf16[64,4,2048]{2,1,0:T(4,128)(2,1)} %reshape.88), channel_id=1, replica_groups=mesh['expert'=64,'cuts'=2,'dp'=8] {'expert'}, dimensions={0} | all-to-all | bytes 2097152 | tf_op jit(solution)/shard_map/all_to_all | solution.py:46
  86.4 1.3 reshape.89
  87.8 6.7 %collective-permute-start = (bf16[256,2048]{1,0:T(8,128)(2,1)S(1)}, bf16[256,2048]{1,0:T(8,128)(2,1)S(1)}, u32[]{:S(2)}, u32[]{:S(2)}) collective-permute-start(bf16[256,2048]{1,0:T(8,128)(2,1)S(1)} %reshape.89), channel_id=1, source_target_pairs={{0,8},{8,0},{1,9},{9,1},{2,10},{10,2},{3,11},{11,3},{4,12},{12,4},... | collective-permute-start | bytes 3145736 | tf_op jit(solution)/shard_map/ppermute | solution.py:49
  94.5 2.3 %collective-permute-done = bf16[256,2048]{1,0:T(8,128)(2,1)S(1)} collective-permute-done((bf16[256,2048]{1,0:T(8,128)(2,1)S(1)}, bf16[256,2048]{1,0:T(8,128)(2,1)S(1)}, u32[]{:S(2)}, u32[]{:S(2)}) %collective-permute-start) | collective-permute-done | bytes 1048608 | tf_op jit(solution)/shard_map/ppermute | solution.py:49
  100.7 1.6 copy.100
  102.2 0.8 multiply_convert_fusion.1
  103.0 1.9 convolution_convert_fusion.1
  104.9 2.6 %copy.98 = bf16[2048,384]{0,1:T(8,128)(2,1)} copy(bf16[2048,384]{1,0:T(8,128)(2,1)} %convolution_convert_fusion.1) | data formatting | bytes 3145728 | tf_op jit(solution)/shard_map/convert_element_type | solution.py:81
  107.5 3.1 %copy.108 = bf16[48,8,8,256]{3,2,1,0:T(8,128)(2,1)} copy(bf16[48,8,8,256]{3,1,2,0:T(8,128)(2,1)} %bitcast.70) | data formatting | bytes 3145728
  110.6 2.9 %copy.99 = bf16[8,3,256,128]{3,2,1,0:T(8,128)(2,1)} copy(bf16[8,3,256,128]{2,0,3,1:T(8,128)(2,1)} %bitcast.71) | data formatting | bytes 3145728 | tf_op jit(solution)/shard_map/transpose | solution.py:75
  113.4 1.9 convolution_convert_fusion.2
  115.3 1.7 copy.96
  117.0 1.7 copy.107
  118.7 3.0 %copy.97 = bf16[8,3,256,128]{3,2,1,0:T(8,128)(2,1)} copy(bf16[8,3,256,128]{2,0,3,1:T(8,128)(2,1)} %bitcast.73) | data formatting | bytes 3145728 | tf_op jit(solution)/shard_map/transpose | solution.py:75
  121.7 3.7 %pad_maximum_fusion = bf16[8,2304,128]{2,1,0:T(8,128)(2,1)} fusion(bf16[8,768,128]{2,1,0:T(8,128)(2,1)S(1)} %bitcast.66, bf16[8,768,128]{2,1,0:T(8,128)(2,1)} %bitcast.67, bf16[8,768,128]{2,1,0:T(8,128)(2,1)} %bitcast.68), kind=kLoop, calls=%fused_computation | loop fusion | flops 14155776 | bytes 9437184 | tf_op jit(solution)/shard_map/concatenate | solution.py:84
  125.4 0.7 fusion
  126.8 0.8 convolution_add_fusion
  127.7 3.5 %collective-permute-start.1 = (bf16[256,1024]{1,0:T(8,128)(2,1)S(1)}, bf16[256,1024]{1,0:T(8,128)(2,1)S(1)}, u32[]{:S(2)}, u32[]{:S(2)}) collective-permute-start(bf16[256,1024]{1,0:T(8,128)(2,1)S(1)} %select_convert_fusion), channel_id=1, source_target_pairs={{0,8},{8,0},{1,9},{9,1},{2,10},{10,2},{3,11},{11,3},{4,12},{12,4},... | collective-permute-start | bytes 1572872 | tf_op jit(solution)/shard_map/ppermute | solution.py:90
  131.2 1.5 collective-permute-done.1
  133.0 1.0 reshape.90
  134.1 5.6 %all-to-all-start.1 = ((bf16[64,4,1024]{2,1,0:T(4,128)(2,1)}), bf16[64,4,1024]{2,1,0:T(4,128)(2,1)S(1)}, u32[]{:S(2)}, u32[]{:S(2)}) async-start(bf16[64,4,1024]{2,1,0:T(4,128)(2,1)} %reshape.90), calls=%async_computation.1 | async-start | bytes 1048576 | tf_op jit(solution)/shard_map/all_to_all | solution.py:91
  139.6 31.0 %all-to-all-done.1 = bf16[64,4,1024]{2,1,0:T(4,128)(2,1)S(1)} async-done(((bf16[64,4,1024]{2,1,0:T(4,128)(2,1)}), bf16[64,4,1024]{2,1,0:T(4,128)(2,1)S(1)}, u32[]{:S(2)}, u32[]{:S(2)}) %all-to-all-start.1) | async-done | bytes 524320 | tf_op jit(solution)/shard_map/all_to_all | solution.py:91
  170.6 0.9 fusion.10
  171.5 14.4 %reduce-scatter.2.cloned.1.call-done = bf16[1,2304,128]{2,1,0:T(8,128)(2,1)} async-done(((bf16[8,2304,128]{2,1,0:T(8,128)(2,1)}), bf16[1,2304,128]{2,1,0:T(8,128)(2,1)}) %reduce-scatter.2.cloned.1.call-update) | async-done | bytes 589840 | tf_op jit(solution)/shard_map/reduce_scatter | solution.py:85
  185.8 1.2 fusion.39
  187.2 0.8 copy.104
  188.1 0.8 copy.105
  189.0 0.8 reshape.102
  (39 shorter events, 6.4 us)
Async XLA Ops:
  7.2 89.7 %copy-start = (bf16[2048,1,384]{2,0,1:T(8,128)(2,1)S(1)}, bf16[2048,1,384]{2,0,1:T(8,128)(2,1)}, u32[]{:S(2)}) copy-start(bf16[2048,1,384]{2,0,1:T(8,128)(2,1)} %param.11) | copy-start | bytes 4718596
  7.2 178.7 %reduce-scatter.2.cloned.1.call-start = ((), (), s32[]{:S(2)}) async-start(), calls=%async_computation.3 | async-start | bytes 5308416 | tf_op jit(solution)/shard_map/reduce_scatter | solution.py:85
  87.8 6.7 %copy-start.4 = (bf16[256,2048]{1,0:T(8,128)(2,1)}, bf16[256,2048]{1,0:T(8,128)(2,1)S(1)}, u32[]{:S(2)}) copy-start(bf16[256,2048]{1,0:T(8,128)(2,1)S(1)} %reshape.89) | copy-start | bytes 3145732
  87.8 9.0 %collective-permute-start = (bf16[256,2048]{1,0:T(8,128)(2,1)S(1)}, bf16[256,2048]{1,0:T(8,128)(2,1)S(1)}, u32[]{:S(2)}, u32[]{:S(2)}) collective-permute-start(bf16[256,2048]{1,0:T(8,128)(2,1)S(1)} %reshape.89), channel_id=1, source_target_pairs={{0,8},{8,0},{1,9},{9,1},{2,10},{10,2},{3,11},{11,3},{4,12},{12,4},... | collective-permute-start | bytes 3145736 | tf_op jit(solution)/shard_map/ppermute | solution.py:49
  96.9 1.4 copy-start.2
  98.3 1.2 copy-start.5
  100.7 1.6 copy-start.6
  118.7 3.0 %copy-start.1 = (bf16[8,48,16,128]{3,1,2,0:T(8,128)(2,1)S(1)}, bf16[8,48,16,128]{3,1,2,0:T(8,128)(2,1)}, u32[]{:S(2)}) copy-start(bf16[8,48,16,128]{3,1,2,0:T(8,128)(2,1)} %copy.100) | copy-start | bytes 4718596
  125.4 1.4 copy-start.3
  127.7 5.0 %collective-permute-start.1 = (bf16[256,1024]{1,0:T(8,128)(2,1)S(1)}, bf16[256,1024]{1,0:T(8,128)(2,1)S(1)}, u32[]{:S(2)}, u32[]{:S(2)}) collective-permute-start(bf16[256,1024]{1,0:T(8,128)(2,1)S(1)} %select_convert_fusion), channel_id=1, source_target_pairs={{0,8},{8,0},{1,9},{9,1},{2,10},{10,2},{3,11},{11,3},{4,12},{12,4},... | collective-permute-start | bytes 1572872 | tf_op jit(solution)/shard_map/ppermute | solution.py:90
  134.1 36.5 %all-to-all-start.1 = ((bf16[64,4,1024]{2,1,0:T(4,128)(2,1)}), bf16[64,4,1024]{2,1,0:T(4,128)(2,1)S(1)}, u32[]{:S(2)}, u32[]{:S(2)}) async-start(bf16[64,4,1024]{2,1,0:T(4,128)(2,1)} %reshape.90), calls=%async_computation.1 | async-start | bytes 1048576 | tf_op jit(solution)/shard_map/all_to_all | solution.py:91
Sparse Core Ops, SparseCore 0:
  125.5 60.2 reduce-scatter.1

commit v2 on v1

v2 whole, which is shorter than its diff:
```python
import functools

import jax
import jax.numpy as jnp
from jax import lax
from jax.experimental import pallas as pl
from jax.experimental.pallas import tpu as pltpu
from jax.sharding import PartitionSpec as P

EXPERTS = 64
CAP = 4
SLOTS = EXPERTS * CAP
VMEM = pl.BlockSpec(memory_space=pltpu.VMEM)
SMEM = pl.BlockSpec(memory_space=pltpu.SMEM)
ANY = pl.BlockSpec(memory_space=pl.ANY)
PARAMS = pltpu.CompilerParams(vmem_limit_bytes=32 * 1024 * 1024)


def dot(a, b, da, db, precision=None):
    return lax.dot_general(
        a, b, (((da,), (db,)), ((), ())), precision=precision, preferred_element_type=jnp.float32
    )


def send_kernel(cut, ids, probs, tokens, grads, sent, picked):
    rows, top = ids.shape
    lane = lax.broadcasted_iota(jnp.int32, (rows, SLOTS), 1)
    expert = lax.shift_right_logical(lane, 2)
    names = jnp.zeros((rows, SLOTS), jnp.float32)
    weight = jnp.zeros((rows, SLOTS), jnp.float32)
    for k in range(top):
        same = ids[:, k : k + 1] == expert
        names = names + jnp.where(same, 1.0, 0.0)
        weight = weight + jnp.where(same, probs[:, k : k + 1], 0.0)
    before = lax.broadcasted_iota(jnp.int32, (rows, rows), 0) > lax.broadcasted_iota(
        jnp.int32, (rows, rows), 1
    )
    rank = dot(jnp.where(before, 1.0, 0.0).astype(jnp.bfloat16), names.astype(jnp.bfloat16), 1, 0)
    place = jnp.bitwise_and(lane, CAP - 1).astype(jnp.float32)
    hit = jnp.where(rank == place, names, 0.0)
    picked[...] = hit.astype(jnp.bfloat16)

    @pl.when(cut[0] == 0)
    def _():
        sent[...] = dot(hit.astype(jnp.bfloat16), tokens[...], 0, 0).astype(jnp.bfloat16)

    @pl.when(cut[0] != 0)
    def _():
        sent[...] = dot(
            hit * weight, grads[...].astype(jnp.float32), 0, 0, lax.Precision.HIGHEST
        ).astype(jnp.bfloat16)


def expert_kernel(
    cut, own, peer, gate_hbm, up_hbm, down_hbm, flat, backs, rows, grads, gate, up, down, sems
):
    def copies(rows_from, grads_from):
        pairs = ((rows_from, rows), (gate_hbm, gate), (up_hbm, up), (grads_from, grads), (down_hbm, down))
        return [pltpu.make_async_copy(a, b, sems.at[i]) for i, (a, b) in enumerate(pairs)]

    @pl.when(cut[0] == 0)
    def _():
        for copy in copies(own, peer):
            copy.start()

    @pl.when(cut[0] != 0)
    def _():
        for copy in copies(peer, own):
            copy.start()

    waits = copies(own, peer)
    for copy in waits[:2]:
        copy.wait()
    gate_val = dot(rows[...], gate[...], 1, 0)
    waits[2].wait()
    up_val = dot(rows[...], up[...], 1, 0)
    sigma = 1.0 / (1.0 + jnp.exp(-gate_val))
    activated = gate_val * sigma
    slope = sigma * (1.0 + gate_val * (1.0 - sigma))
    hidden = activated * up_val
    for copy in waits[3:]:
        copy.wait()
    back_hid = dot(grads[...], down[...], 1, 1)
    gate_back = back_hid * up_val * slope
    up_back = back_hid * activated
    width = rows.shape[1]
    units = hidden.shape[1]
    both = jnp.concatenate((gate_back, up_back), axis=1)
    backs[...] = both.astype(jnp.bfloat16)
    both_t = both.T.astype(jnp.bfloat16)
    hidden_t = hidden.T.astype(jnp.bfloat16)
    replicas = flat.shape[0]
    strip = units // replicas
    share = width // replicas
    for i in range(replicas):
        columns = slice(i * share, (i + 1) * share)
        two = dot(both_t, rows[:, columns], 1, 0).astype(jnp.bfloat16)
        three = dot(hidden_t, grads[:, columns], 1, 0).astype(jnp.bfloat16)
        per = share // 128
        for h in range(per):
            lanes = slice(h * 128, (h + 1) * 128)
            flat[i, h * 2 * units : (h + 1) * 2 * units, :] = two[:, lanes]
            start = 2 * per * units + (i * per + h) * strip
            for j in range(replicas):
                flat[j, start : start + strip, :] = three[j * strip : (j + 1) * strip, lanes]


def rows_kernel(cut, backs, gate, up, mine, other):
    half = mine.shape[1]
    units = gate.shape[1]

    def part(c):
        at = pl.ds(pl.multiple_of(c * half, half), half)
        return dot(backs[:, :units], gate[at, :], 1, 1) + dot(backs[:, units:], up[at, :], 1, 1)

    other[...] = part(1 - cut[0]).astype(jnp.bfloat16)
    mine[...] = part(cut[0])


def unpack_kernel(total, gate, up, down):
    units = gate.shape[1]
    per = gate.shape[0] // 128
    strip = down.shape[0]
    for h in range(per):
        at = h * 2 * units
        lanes = slice(h * 128, (h + 1) * 128)
        gate[lanes, :] = total[at : at + units, :].astype(jnp.float32).T.astype(jnp.bfloat16)
        up[lanes, :] = total[at + units : at + 2 * units, :].astype(jnp.float32).T.astype(jnp.bfloat16)
    base = per * 2 * units
    for j in range(down.shape[1] // 128):
        down[:, j * 128 : (j + 1) * 128] = total[base + j * strip : base + (j + 1) * strip, :]


def shards(tokens, out_grad, expert_ids, route_probs, gate_weight, up_weight, down_weight):
    rows, width = tokens.shape
    half = width // 2
    units = gate_weight.shape[2]
    replicas = lax.axis_size("dp")
    share = width // replicas
    strip = units // replicas
    cut = lax.axis_index("cuts").astype(jnp.int32).reshape(1)
    first = cut[0] == 0
    swap = [(0, 1), (1, 0)]
    w_gate, w_up, w_down = gate_weight[:, 0, :], up_weight[:, 0, :], down_weight[:, 0, :]
    bf16 = functools.partial(jax.ShapeDtypeStruct, dtype=jnp.bfloat16)

    sent, picked = pl.pallas_call(
        send_kernel,
        out_shape=(bf16((SLOTS, width)), bf16((rows, SLOTS))),
        in_specs=[SMEM] + [VMEM] * 4,
        out_specs=(VMEM, VMEM),
        compiler_params=PARAMS,
        name="send",
    )(cut, expert_ids, route_probs, tokens, out_grad)
    own = lax.all_to_all(
        sent.reshape(EXPERTS, CAP, width), "expert", split_axis=0, concat_axis=0, tiled=True
    ).reshape(SLOTS, width)
    peer = lax.ppermute(own, "cuts", swap)

    flat, backs = pl.pallas_call(
        expert_kernel,
        out_shape=(bf16((replicas, 3 * units * share // 128, 128)), bf16((SLOTS, 2 * units))),
        in_specs=[SMEM] + [ANY] * 5,
        out_specs=(VMEM, VMEM),
        scratch_shapes=[
            pltpu.VMEM((SLOTS, width), jnp.bfloat16),
            pltpu.VMEM((SLOTS, width), jnp.bfloat16),
            pltpu.VMEM((width, units), jnp.bfloat16),
            pltpu.VMEM((width, units), jnp.bfloat16),
            pltpu.VMEM((units, width), jnp.bfloat16),
            pltpu.SemaphoreType.DMA((5,)),
        ],
        compiler_params=PARAMS,
        name="expert",
    )(cut, own, peer, w_gate, w_up, w_down)
    total = lax.psum_scatter(flat, "dp", scatter_dimension=0, tiled=True)[0]

    mine, other = pl.pallas_call(
        rows_kernel,
        out_shape=(jax.ShapeDtypeStruct((SLOTS, half), jnp.float32), bf16((SLOTS, half))),
        in_specs=[SMEM] + [VMEM] * 3,
        out_specs=(VMEM, VMEM),
        compiler_params=PARAMS,
        name="rows",
    )(cut, backs, w_gate, w_up)
    mine = mine + lax.ppermute(other, "cuts", swap).astype(jnp.float32)
    returned = lax.all_to_all(
        mine.astype(jnp.bfloat16).reshape(EXPERTS, CAP, half),
        "expert", split_axis=0, concat_axis=0, tiled=True,
    ).reshape(SLOTS, half)
    result = dot(picked, returned, 1, 0).astype(jnp.bfloat16)

    gate_grad, up_grad, down_grad = pl.pallas_call(
        unpack_kernel,
        out_shape=(bf16((share, units)), bf16((share, units)), bf16((strip, width))),
        in_specs=[VMEM],
        out_specs=(VMEM,) * 3,
        compiler_params=PARAMS,
        name="unpack",
    )(total)
    return (result, gate_grad[:, None, :], up_grad[:, None, :], down_grad[:, None, :])


def solution(mesh):
    placed = (
        P(("expert", "dp"), None),
        P(("expert", "dp"), None),
        P(("expert", "dp"), None),
        P(("expert", "dp"), None),
        P(None, "expert", "cuts"),
        P(None, "expert", "cuts"),
        P("cuts", "expert", None),
    )
    return jax.shard_map(
        shards,
        mesh=mesh,
        in_specs=placed,
        out_specs=(
            P(("expert", "dp"), "cuts"),
            P("dp", "expert", "cuts"),
            P("dp", "expert", "cuts"),
            P(("cuts", "dp"), "expert", None),
        ),
        check_vma=False,
    )
```

time: 197 us -> 176 us (0.89)
  blocking collectives: 74.3 us -> 114 us
  waiting for transfers between devices: 49.1 us -> 20.5 us
  local copies, waits for them, and re-layouts: 28.2 us -> 12.1 us
  starting transfers between devices: 15.8 us -> 6.08 us
  matrix products: 9.66 us -> 0.81 us
  Pallas kernels: 0 us -> 8.41 us
  other arithmetic: 5.23 us -> 0.15 us
    all_to_all x0 -> x1, blocking collectives: none -> 36.3 us  [shards(): lax.all_to_all(mine.astype(jnp.bfloat16).reshape(EXPERTS, CAP, half), 'ex...]
    all_to_all x1 -> x0, waiting for transfers between devices: 31 us -> none  [shards(): lax.all_to_all(mine.astype(jnp.bfloat16).reshape(EXPERTS, CAP, half), 'ex...]
    dot_general x11 -> x1, matrix products: 9.66 us -> 0.81 us  [dot(): lax.dot_general(a, b, (((da,), (db,)), ((), ())), precision=precision, pr...]
    pallas_call x0 -> x4, Pallas kernels: none -> 8.41 us  [the longest x1 4.1 us: shards(): pl.pallas_call(expert_kernel, out_shape=(bf16((replicas, 3 * units * shar...]
    transpose x6 -> x0, local copies, waits for them, and re-layouts: 6.32 us -> none  [the longest x2 5.89 us: packed(): return grad.reshape(replicas, share, tiles, 128).transpose(0, 2, 1, 3)]
    all_to_all x1 -> x0, starting transfers between devices: 5.55 us -> none  [shards(): lax.all_to_all(mine.astype(jnp.bfloat16).reshape(EXPERTS, CAP, half), 'ex...]
    convert_element_type x2 -> x0, local copies, waits for them, and re-layouts: 4.31 us -> none  [the longest x1 2.61 us: shards(): dot(rows_in, up_back, 0, 0).astype(jnp.bfloat16)]
    concatenate x1 -> x0, other arithmetic: 3.67 us -> none  [shards(): jnp.concatenate([part.reshape(replicas, tiles * share, 128) for part in p...]
  transfers between devices with their start and end apart: 4 -> 3, of which waited for: 4 -> 3; matrix products, arithmetic and copies ran while one was open for 2% -> 1% of each run, Pallas kernels for 0% -> 1%
where the time goes in v2:
time: 176 us
  blocking collectives  114 us (65%)
  waiting for transfers between devices  20.5 us (12%)
  between operations  14.1 us (8%)
  local copies, waits for them, and re-layouts  12.1 us (7%)
  Pallas kernels  8.41 us (5%)
  starting transfers between devices  6.08 us (3%)
    all_to_all x1, blocking collectives, shards(): lax.all_to_all(sent.reshape(EXPERTS, CAP, width), 'expert', split_axis=0,...  77.2 us
    all_to_all x1, blocking collectives, shards(): lax.all_to_all(mine.astype(jnp.bfloat16).reshape(EXPERTS, CAP, half), 'ex...  36.3 us
    reduce_scatter x1, waiting for transfers between devices, shards(): total = lax.psum_scatter(flat, 'dp', scatter_dimension=0, tiled=True)[0]  16.5 us
    unnamed x18, local copies, waits for them, and re-layouts  9.13 us
    pallas_call x1, Pallas kernels, shards(): pl.pallas_call(expert_kernel, out_shape=(bf16((replicas, 3 * units * shar...  4.1 us
    ppermute x1, starting transfers between devices, shards(): peer = lax.ppermute(own, 'cuts', swap)  3.75 us
  transfers between devices with their start and end apart: 3, of which 3 were waited for; matrix products, arithmetic and copies ran while one was open for 1% of the time, Pallas kernels for 1%

profile of v2, /device:TPU:1, one launch (start us, length us, event | category | flops | bytes accessed | tf_op | source)
XLA Modules:
  0.0 175.7 jit_solution(16050177556404558184)
XLA Ops:
  7.2 0.0 reduce-scatter.2.cloned.1.call-start
  7.2 0.8 copy.11.ids
  8.0 0.8 copy.12.probs
  8.7 0.0 copy-start.6
  8.7 0.9 copy-done.6
  9.6 0.9 copy-done.7
  10.5 2.1 %send.1 = (bf16[256,2048]{1,0:T(8,128)(2,1)S(1)}, bf16[24,256]{1,0:T(8,128)(2,1)S(1)}) custom-call(s32[1]{0:T(128)} %bitcast.cut, s32[24,8]{1,0:T(8,128)S(1)} %copy.11.ids, f32[24,8]{1,0:T(8,128)S(1)} %copy.12.probs, bf16[24,2048]{1,0:T(8,128)(2,1)S(1)} %copy-done.6, bf16[24,2048]{1,0:T(8,128)(2,1)S(1)} %copy-done.7), custom_call_target="tpu_custom_call" | custom-call | tf_op jit(solution)/shard_map/send/pallas_call | solution.py:147
  12.6 0.4 reshape.24
  13.0 0.0 copy-start.1
  13.0 77.2 %all_to_all.10 = bf16[64,4,2048]{2,1,0:T(4,128)(2,1)} all-to-all(bf16[64,4,2048]{2,1,0:T(4,128)(2,1)S(1)} %reshape.24), channel_id=1, replica_groups=mesh['expert'=64,'cuts'=2,'dp'=8] {'expert'}, dimensions={0} | all-to-all | bytes 2097152 | tf_op jit(solution)/shard_map/all_to_all | solution.py:155
  90.2 2.3 %reshape.25.own = bf16[256,2048]{1,0:T(8,128)(2,1)} reshape(bf16[64,4,2048]{2,1,0:T(4,128)(2,1)} %all_to_all.10) | data formatting | bytes 2097152 | tf_op jit(solution)/shard_map/reshape | solution.py:157
  92.5 3.7 %collective-permute-start = (bf16[256,2048]{1,0:T(8,128)(2,1)}, bf16[256,2048]{1,0:T(8,128)(2,1)S(1)}, u32[]{:S(2)}, u32[]{:S(2)}) collective-permute-start(bf16[256,2048]{1,0:T(8,128)(2,1)} %reshape.25.own), channel_id=1, source_target_pairs={{0,8},{8,0},{1,9},{9,1},{2,10},{10,2},{3,11},{11,3},{4,12},{12,4},... | collective-permute-start | bytes 3145736 | tf_op jit(solution)/shard_map/ppermute | solution.py:158
  96.3 2.5 %collective-permute-done.peer = bf16[256,2048]{1,0:T(8,128)(2,1)S(1)} collective-permute-done((bf16[256,2048]{1,0:T(8,128)(2,1)}, bf16[256,2048]{1,0:T(8,128)(2,1)S(1)}, u32[]{:S(2)}, u32[]{:S(2)}) %collective-permute-start) | collective-permute-done | bytes 1048608 | tf_op jit(solution)/shard_map/ppermute | solution.py:158
  98.8 0.0 copy-done.1
  98.8 0.0 copy-done
  98.8 1.2 copy-done.3
  100.0 1.4 copy-done.4
  101.4 4.1 %expert.1 = (bf16[8,2304,128]{2,1,0:T(8,128)(2,1)S(1)}, bf16[256,768]{1,0:T(8,128)(2,1)S(1)}) custom-call(s32[1]{0:T(128)} %bitcast.cut, bf16[256,2048]{1,0:T(8,128)(2,1)S(1)} %copy-done.3, bf16[256,2048]{1,0:T(8,128)(2,1)S(1)} %collective-permute-done.peer, bf16[2048,384]{1,0:T(8,128)(2,1)S(1)} %bitcast.10, bf16[2048,384]{1,0:T(8,128)(2,1)S(1)} %bitcast.12, ...), custom_call_target="tpu_custom_call" | custom-call | tf_op jit(solution)/shard_map/expert/pallas_call | solution.py:160
  105.5 0.0 copy-start.2
  105.5 2.1 %copy-done.2 = bf16[8,2304,128]{2,1,0:T(8,128)(2,1)} copy-done((bf16[8,2304,128]{2,1,0:T(8,128)(2,1)}, bf16[8,2304,128]{2,1,0:T(8,128)(2,1)S(1)}, u32[]{:S(2)}) %copy-start.2) | copy-done | bytes 4718616
  107.6 0.0 reduce-scatter.2.cloned.1.call-update
  107.6 1.3 rows.1
  108.9 2.3 %collective-permute-start.1 = (bf16[256,1024]{1,0:T(8,128)(2,1)S(1)}, bf16[256,1024]{1,0:T(8,128)(2,1)S(1)}, u32[]{:S(2)}, u32[]{:S(2)}) collective-permute-start(bf16[256,1024]{1,0:T(8,128)(2,1)S(1)} %get-tuple-element.17), channel_id=1, source_target_pairs={{0,8},{8,0},{1,9},{9,1},{2,10},{10,2},{3,11},{11,3},{4,12},{12,4},... | collective-permute-start | bytes 1572872 | tf_op jit(solution)/shard_map/ppermute | solution.py:186
  111.2 1.5 collective-permute-done.1
  112.7 0.1 add_convert_fusion
  112.9 0.2 reshape.26
  113.1 36.3 %all_to_all.11 = bf16[64,4,1024]{2,1,0:T(4,128)(2,1)S(1)} all-to-all(bf16[64,4,1024]{2,1,0:T(4,128)(2,1)S(1)} %reshape.26), channel_id=1, replica_groups=mesh['expert'=64,'cuts'=2,'dp'=8] {'expert'}, dimensions={0} | all-to-all | bytes 1048576 | tf_op jit(solution)/shard_map/all_to_all | solution.py:187
  149.4 0.1 reshape.27
  149.6 0.8 convolution_convert_fusion
  150.4 16.5 %reduce-scatter.2.cloned.1.call-done = bf16[1,2304,128]{2,1,0:T(8,128)(2,1)} async-done(((bf16[8,2304,128]{2,1,0:T(8,128)(2,1)}), bf16[1,2304,128]{2,1,0:T(8,128)(2,1)}) %reduce-scatter.2.cloned.1.call-update) | async-done | bytes 589840 | tf_op jit(solution)/shard_map/reduce_scatter | solution.py:176
  166.8 1.1 copy-done.5
  167.9 1.0 unpack.1
  (5 shorter events, 0.0 us)
Async XLA Ops:
  7.2 159.7 %reduce-scatter.2.cloned.1.call-start = ((), (), s32[]{:S(2)}) async-start(), calls=%async_computation.3 | async-start | bytes 5308416 | tf_op jit(solution)/shard_map/reduce_scatter | solution.py:176
  8.7 0.9 copy-start.6
  9.6 0.9 copy-start.7
  13.0 85.7 %copy-start.1 = (bf16[2048,1,384]{2,0,1:T(8,128)(2,1)S(1)}, bf16[2048,1,384]{2,0,1:T(8,128)(2,1)}, u32[]{:S(2)}) copy-start(bf16[2048,1,384]{2,0,1:T(8,128)(2,1)} %param.12) | copy-start | bytes 4718596
  90.2 8.5 %copy-start = (bf16[2048,1,384]{2,0,1:T(8,128)(2,1)S(1)}, bf16[2048,1,384]{2,0,1:T(8,128)(2,1)}, u32[]{:S(2)}) copy-start(bf16[2048,1,384]{2,0,1:T(8,128)(2,1)} %param.11) | copy-start | bytes 4718596
  92.5 6.2 %collective-permute-start = (bf16[256,2048]{1,0:T(8,128)(2,1)}, bf16[256,2048]{1,0:T(8,128)(2,1)S(1)}, u32[]{:S(2)}, u32[]{:S(2)}) collective-permute-start(bf16[256,2048]{1,0:T(8,128)(2,1)} %reshape.25.own), channel_id=1, source_target_pairs={{0,8},{8,0},{1,9},{9,1},{2,10},{10,2},{3,11},{11,3},{4,12},{12,4},... | collective-permute-start | bytes 3145736 | tf_op jit(solution)/shard_map/ppermute | solution.py:158
  98.8 1.2 copy-start.3
  100.0 1.4 copy-start.4
  105.5 2.1 %copy-start.2 = (bf16[8,2304,128]{2,1,0:T(8,128)(2,1)}, bf16[8,2304,128]{2,1,0:T(8,128)(2,1)S(1)}, u32[]{:S(2)}) copy-start(bf16[8,2304,128]{2,1,0:T(8,128)(2,1)S(1)} %get-tuple-element.18) | copy-start | bytes 14155780
  108.9 3.8 %collective-permute-start.1 = (bf16[256,1024]{1,0:T(8,128)(2,1)S(1)}, bf16[256,1024]{1,0:T(8,128)(2,1)S(1)}, u32[]{:S(2)}, u32[]{:S(2)}) collective-permute-start(bf16[256,1024]{1,0:T(8,128)(2,1)S(1)} %get-tuple-element.17), channel_id=1, source_target_pairs={{0,8},{8,0},{1,9},{9,1},{2,10},{10,2},{3,11},{11,3},{4,12},{12,4},... | collective-permute-start | bytes 1572872 | tf_op jit(solution)/shard_map/ppermute | solution.py:186
  166.8 1.1 copy-start.5
Sparse Core Ops, SparseCore 0:
  107.8 59.0 reduce-scatter.1

commit v3 on v2

v3 whole, which is shorter than its diff:
```python
import functools

import jax
import jax.numpy as jnp
from jax import lax
from jax.experimental import pallas as pl
from jax.experimental.pallas import tpu as pltpu
from jax.sharding import PartitionSpec as P

EXPERTS = 64
CAP = 4
SLOTS = EXPERTS * CAP
VMEM = pl.BlockSpec(memory_space=pltpu.VMEM)
SMEM = pl.BlockSpec(memory_space=pltpu.SMEM)
ANY = pl.BlockSpec(memory_space=pl.ANY)
HBM = pl.BlockSpec(memory_space=pltpu.HBM)
PARAMS = pltpu.CompilerParams(vmem_limit_bytes=32 * 1024 * 1024)


def dot(a, b, da, db, precision=None):
    return lax.dot_general(
        a, b, (((da,), (db,)), ((), ())), precision=precision, preferred_element_type=jnp.float32
    )


def pack_kernel(cut, ids_hbm, probs_hbm, tokens, grads, packed, ids_t, probs_t, sems):
    top = ids_t.shape[0]
    width = tokens.shape[1]
    body = packed.at[:, pl.ds(0, width)]
    load_ids = pltpu.make_async_copy(ids_hbm, ids_t, sems.at[0])
    load_probs = pltpu.make_async_copy(probs_hbm, probs_t, sems.at[1])
    load_ids.start()
    load_probs.start()

    @pl.when(cut[0] == 0)
    def _():
        pltpu.make_async_copy(tokens, body, sems.at[2]).start()

    @pl.when(cut[0] != 0)
    def _():
        pltpu.make_async_copy(grads, body, sems.at[2]).start()

    load_ids.wait()
    load_probs.wait()
    probs = probs_t[...]
    high = probs.astype(jnp.bfloat16).astype(jnp.float32)
    middle = (probs - high).astype(jnp.bfloat16).astype(jnp.float32)
    low = probs - high - middle
    terms = jnp.concatenate((ids_t[...].astype(jnp.float32), high, middle, low), axis=0)
    row = lax.broadcasted_iota(jnp.int32, (4 * top, 128), 0)
    unit = jnp.where(row == lax.broadcasted_iota(jnp.int32, (4 * top, 128), 1), 1.0, 0.0)
    packed[:, width:] = dot(
        terms.astype(jnp.bfloat16), unit.astype(jnp.bfloat16), 0, 0
    ).astype(jnp.bfloat16)
    pltpu.make_async_copy(tokens, body, sems.at[2]).wait()


def ranks(names):
    rows = names.shape[0]
    before = lax.broadcasted_iota(jnp.int32, (rows, rows), 0) > lax.broadcasted_iota(
        jnp.int32, (rows, rows), 1
    )
    return dot(jnp.where(before, 1.0, 0.0).astype(jnp.bfloat16), names.astype(jnp.bfloat16), 1, 0)


def pick_kernel(place, own, behind, ahead, across, sent):
    rows, packed = own.shape
    width = sent.shape[1]
    f32 = jnp.float32
    blocks = (own, behind, ahead, across)
    source = jnp.concatenate([b[:, :width].astype(f32) for b in blocks], axis=0).astype(jnp.bfloat16)
    facts = jnp.concatenate([b[:, width:].astype(f32) for b in blocks], axis=0)
    total = 4 * rows
    group = place[1]
    token = lax.broadcasted_iota(jnp.int32, (total, SLOTS), 0)
    lane = lax.broadcasted_iota(jnp.int32, (total, SLOTS), 1)
    shift = jnp.where(
        token < rows, 0, jnp.where(token < 2 * rows, 3, jnp.where(token < 3 * rows, 1, 2))
    )
    block = jnp.bitwise_and(group + shift, 3)
    here = block == jnp.bitwise_and(lax.shift_right_logical(lane, 2), 3)
    expert = (group * 16 + lax.shift_right_logical(lane, 4)).astype(f32)
    names = jnp.zeros((total, SLOTS), f32)
    weight = jnp.zeros((total, SLOTS), f32)
    top = 8
    prob = facts[:, top : 2 * top] + facts[:, 2 * top : 3 * top] + facts[:, 3 * top : 4 * top]
    for k in range(top):
        same = jnp.logical_and(facts[:, k : k + 1] == expert, here)
        names = names + jnp.where(same, 1.0, 0.0)
        weight = weight + jnp.where(same, prob[:, k : k + 1], 0.0)
    slot = jnp.bitwise_and(lane, CAP - 1).astype(f32)
    hit = jnp.where(ranks(names) == slot, names, 0.0)

    @pl.when(place[0] == 0)
    def _():
        sent[...] = dot(hit.astype(jnp.bfloat16), source, 0, 0).astype(jnp.bfloat16)

    @pl.when(place[0] != 0)
    def _():
        factor = hit * weight
        high = factor.astype(jnp.bfloat16)
        middle = (factor - high.astype(f32)).astype(jnp.bfloat16)
        low = (factor - high.astype(f32) - middle.astype(f32)).astype(jnp.bfloat16)
        sent[...] = (
            dot(high, source, 0, 0) + (dot(middle, source, 0, 0) + dot(low, source, 0, 0))
        ).astype(jnp.bfloat16)


def combine_kernel(ids_t, returned, out):
    top, rows = ids_t.shape
    unit = jnp.where(
        lax.broadcasted_iota(jnp.int32, (top, top), 0) == lax.broadcasted_iota(jnp.int32, (top, top), 1),
        1.0, 0.0,
    )
    ids = dot(ids_t[...].astype(jnp.bfloat16), unit.astype(jnp.bfloat16), 0, 0)
    lane = lax.broadcasted_iota(jnp.int32, (rows, SLOTS), 1)
    expert = lax.shift_right_logical(lane, 2).astype(jnp.float32)
    names = jnp.zeros((rows, SLOTS), jnp.float32)
    for k in range(top):
        names = names + jnp.where(ids[:, k : k + 1] == expert, 1.0, 0.0)
    slot = jnp.bitwise_and(lane, CAP - 1).astype(jnp.float32)
    hit = jnp.where(ranks(names) == slot, names, 0.0)
    out[...] = dot(hit.astype(jnp.bfloat16), returned[...], 1, 0).astype(jnp.bfloat16)


def expert_kernel(
    place, own, peer, gate_hbm, up_hbm, down_hbm, flat_hbm, backs,
    rows, grads, gate, up, down, flat, sems, out_sems,
):
    def copies(rows_from, grads_from):
        pairs = ((rows_from, rows), (gate_hbm, gate), (up_hbm, up), (grads_from, grads), (down_hbm, down))
        return [pltpu.make_async_copy(a, b, sems.at[i]) for i, (a, b) in enumerate(pairs)]

    @pl.when(place[0] == 0)
    def _():
        for copy in copies(own, peer):
            copy.start()

    @pl.when(place[0] != 0)
    def _():
        for copy in copies(peer, own):
            copy.start()

    waits = copies(own, peer)
    for copy in waits[:2]:
        copy.wait()
    gate_val = dot(rows[...], gate[...], 1, 0)
    waits[2].wait()
    up_val = dot(rows[...], up[...], 1, 0)
    sigma = 1.0 / (1.0 + jnp.exp(-gate_val))
    activated = gate_val * sigma
    slope = sigma * (1.0 + gate_val * (1.0 - sigma))
    hidden_t = (activated * up_val).T.astype(jnp.bfloat16)
    width = rows.shape[1]
    units = gate.shape[1]
    replicas = flat.shape[0]
    strip = units // replicas
    share = width // replicas
    per = share // 128
    for copy in waits[3:]:
        copy.wait()
    back_hid = dot(grads[...], down[...], 1, 1)
    for i in range(replicas):
        columns = slice(i * share, (i + 1) * share)
        part = dot(hidden_t, grads[:, columns], 1, 0).astype(jnp.bfloat16)
        for h in range(per):
            lanes = slice(h * 128, (h + 1) * 128)
            start = 2 * per * units + (i * per + h) * strip
            for j in range(replicas):
                flat[j, start : start + strip, :] = part[j * strip : (j + 1) * strip, lanes]
    both = jnp.concatenate((back_hid * up_val * slope, back_hid * activated), axis=1)
    backs[...] = both.astype(jnp.bfloat16)
    both_t = both.T.astype(jnp.bfloat16)
    outs = [
        pltpu.make_async_copy(flat.at[i], flat_hbm.at[i], out_sems.at[i]) for i in range(replicas)
    ]
    for i in range(replicas):
        columns = slice(i * share, (i + 1) * share)
        part = dot(both_t, rows[:, columns], 1, 0).astype(jnp.bfloat16)
        for h in range(per):
            flat[i, h * 2 * units : (h + 1) * 2 * units, :] = part[:, h * 128 : (h + 1) * 128]
        outs[i].start()
    for copy in outs:
        copy.wait()


def rows_kernel(cut, backs, gate, up, mine, other):
    half = mine.shape[1]
    units = gate.shape[1]

    def part(c):
        at = pl.ds(pl.multiple_of(c * half, half), half)
        return dot(backs[:, :units], gate[at, :], 1, 1) + dot(backs[:, units:], up[at, :], 1, 1)

    other[...] = part(1 - cut[0]).astype(jnp.bfloat16)
    mine[...] = part(cut[0])


def unpack_kernel(total, gate, up, down):
    units = gate.shape[1]
    per = gate.shape[0] // 128
    strip = down.shape[0]
    for h in range(per):
        at = h * 2 * units
        lanes = slice(h * 128, (h + 1) * 128)
        gate[lanes, :] = total[at : at + units, :].astype(jnp.float32).T.astype(jnp.bfloat16)
        up[lanes, :] = total[at + units : at + 2 * units, :].astype(jnp.float32).T.astype(jnp.bfloat16)
    base = per * 2 * units
    for j in range(down.shape[1] // 128):
        down[:, j * 128 : (j + 1) * 128] = total[base + j * strip : base + (j + 1) * strip, :]


def shards(tokens, out_grad, expert_ids, route_probs, gate_weight, up_weight, down_weight):
    rows, width = tokens.shape
    half = width // 2
    units = gate_weight.shape[2]
    replicas = lax.axis_size("dp")
    share = width // replicas
    strip = units // replicas
    cut = lax.axis_index("cuts").astype(jnp.int32).reshape(1)
    place = jnp.stack((lax.axis_index("cuts"), lax.axis_index("expert") // 16)).astype(jnp.int32)
    swap = [(0, 1), (1, 0)]
    w_gate, w_up, w_down = gate_weight[:, 0, :], up_weight[:, 0, :], down_weight[:, 0, :]
    bf16 = functools.partial(jax.ShapeDtypeStruct, dtype=jnp.bfloat16)
    ids_t, probs_t = expert_ids.T, route_probs.T

    packed = pl.pallas_call(
        pack_kernel,
        out_shape=bf16((rows, width + 128)),
        in_specs=[SMEM] + [ANY] * 4,
        out_specs=VMEM,
        scratch_shapes=[
            pltpu.VMEM(ids_t.shape, jnp.int32),
            pltpu.VMEM(probs_t.shape, jnp.float32),
            pltpu.SemaphoreType.DMA((3,)),
        ],
        compiler_params=pltpu.CompilerParams(vmem_limit_bytes=60 * 1024 * 1024),
        name="pack",
    )(cut, ids_t, probs_t, tokens, out_grad)
    up_by = [(i, (i + 16) % EXPERTS) for i in range(EXPERTS)]
    down_by = [(j, i) for i, j in up_by]
    behind = lax.ppermute(packed, "expert", up_by)
    ahead = lax.ppermute(packed, "expert", down_by)
    across = lax.ppermute(packed, "expert", [(i, (i + 32) % EXPERTS) for i in range(EXPERTS)])
    sent = pl.pallas_call(
        pick_kernel,
        out_shape=bf16((SLOTS, width)),
        in_specs=[SMEM] + [VMEM] * 4,
        out_specs=VMEM,
        compiler_params=PARAMS,
        name="pick",
    )(place, packed, behind, ahead, across)
    quarters = [[q * 16 + i for i in range(16)] for q in range(4)]
    own = lax.all_to_all(
        sent.reshape(16, 4 * CAP, width), "expert", split_axis=0, concat_axis=0, tiled=True,
        axis_index_groups=quarters,
    ).reshape(SLOTS, width)
    peer = lax.ppermute(own, "cuts", swap)

    flat, backs = pl.pallas_call(
        expert_kernel,
        out_shape=(bf16((replicas, 3 * units * share // 128, 128)), bf16((SLOTS, 2 * units))),
        in_specs=[SMEM, HBM] + [ANY] * 4,
        out_specs=(HBM, VMEM),
        scratch_shapes=[
            pltpu.VMEM((SLOTS, width), jnp.bfloat16),
            pltpu.VMEM((SLOTS, width), jnp.bfloat16),
            pltpu.VMEM((width, units), jnp.bfloat16),
            pltpu.VMEM((width, units), jnp.bfloat16),
            pltpu.VMEM((units, width), jnp.bfloat16),
            pltpu.VMEM((replicas, 3 * units * share // 128, 128), jnp.bfloat16),
            pltpu.SemaphoreType.DMA((5,)),
            pltpu.SemaphoreType.DMA((replicas,)),
        ],
        compiler_params=pltpu.CompilerParams(vmem_limit_bytes=48 * 1024 * 1024),
        name="expert",
    )(cut, own, peer, w_gate, w_up, w_down)
    total = lax.psum_scatter(flat, "dp", scatter_dimension=0, tiled=True)[0]

    mine, other = pl.pallas_call(
        rows_kernel,
        out_shape=(jax.ShapeDtypeStruct((SLOTS, half), jnp.float32), bf16((SLOTS, half))),
        in_specs=[SMEM] + [VMEM] * 3,
        out_specs=(VMEM, VMEM),
        compiler_params=PARAMS,
        name="rows",
    )(cut, backs, w_gate, w_up)
    mine = mine + lax.ppermute(other, "cuts", swap).astype(jnp.float32)
    returned = lax.all_to_all(
        mine.astype(jnp.bfloat16).reshape(16, 4, CAP, half).transpose(1, 0, 2, 3)
        .reshape(EXPERTS, CAP, half),
        "expert", split_axis=0, concat_axis=0, tiled=True,
    ).reshape(SLOTS, half)
    result = pl.pallas_call(
        combine_kernel,
        out_shape=bf16((rows, half)),
        in_specs=[VMEM] * 2,
        out_specs=VMEM,
        compiler_params=PARAMS,
        name="combine",
    )(ids_t, returned)

    gate_grad, up_grad, down_grad = pl.pallas_call(
        unpack_kernel,
        out_shape=(bf16((share, units)), bf16((share, units)), bf16((strip, width))),
        in_specs=[VMEM],
        out_specs=(VMEM,) * 3,
        compiler_params=PARAMS,
        name="unpack",
    )(total)
    return (result, gate_grad[:, None, :], up_grad[:, None, :], down_grad[:, None, :])


def solution(mesh):
    placed = (
        P(("expert", "dp"), None),
        P(("expert", "dp"), None),
        P(("expert", "dp"), None),
        P(("expert", "dp"), None),
        P(None, "expert", "cuts"),
        P(None, "expert", "cuts"),
        P("cuts", "expert", None),
    )
    return jax.shard_map(
        shards,
        mesh=mesh,
        in_specs=placed,
        out_specs=(
            P(("expert", "dp"), "cuts"),
            P("dp", "expert", "cuts"),
            P("dp", "expert", "cuts"),
            P(("cuts", "dp"), "expert", None),
        ),
        check_vma=False,
    )
```

time: 176 us -> 171 us (0.972)
  blocking collectives: 114 us -> 74.5 us
  starting transfers between devices: 6.08 us -> 35.4 us
  waiting for transfers between devices: 20.5 us -> 30.8 us
  local copies, waits for them, and re-layouts: 12.1 us -> 2.49 us
  Pallas kernels: 8.41 us -> 12.6 us
    all_to_all x2, blocking collectives: 114 us -> 74.5 us  [the longest x1 43.6 us: shards(): lax.all_to_all(mine.astype(jnp.bfloat16).reshape(16, 4, CAP, half).transp...]
    ppermute x0 -> x3, starting transfers between devices: none -> 29.1 us  [the longest x1 19.9 us: shards(): lax.ppermute(packed, 'expert', [(i, (i + 32) % EXPERTS) for i in range(EX...]
    ppermute x0 -> x3, waiting for transfers between devices: none -> 11.1 us  [the longest x1 11.1 us: shards(): ahead = lax.ppermute(packed, 'expert', down_by)]
    unnamed x18 -> x10, local copies, waits for them, and re-layouts: 9.13 us -> 1.97 us
    pallas_call x1 -> x3, Pallas kernels: 2.05 us -> 4.83 us  [the longest x1 2.05 us: shards(): pl.pallas_call(pick_kernel, out_shape=bf16((SLOTS, width)), in_specs=[SME...]
    reshape x4 -> x2, local copies, waits for them, and re-layouts: 3.02 us -> 0.32 us  [the longest x1 0.2 us: shards(): mine.astype(jnp.bfloat16).reshape(16, 4, CAP, half).transpose(1, 0, 2, 3)]
  transfers between devices with their start and end apart: 3 -> 6, of which waited for: 3 -> 4; matrix products, arithmetic and copies ran while one was open for 1% -> 0% of each run, Pallas kernels for 1% -> 1%
where the time goes in v3:
time: 171 us; the launch traced here: 170 us
  blocking collectives  74.5 us (44%)
  starting transfers between devices  35.4 us (21%)
  waiting for transfers between devices  30.8 us (18%)
  between operations  14.2 us (8%)
  Pallas kernels  12.6 us (7%)
  local copies, waits for them, and re-layouts  2.49 us (1%)
    all_to_all x1, blocking collectives, shards(): lax.all_to_all(mine.astype(jnp.bfloat16).reshape(16, 4, CAP, half).transp...  43.6 us
    all_to_all x1, blocking collectives, shards(): lax.all_to_all(sent.reshape(16, 4 * CAP, width), 'expert', split_axis=0,...  30.9 us
    ppermute x1, starting transfers between devices, shards(): lax.ppermute(packed, 'expert', [(i, (i + 32) % EXPERTS) for i in range(EX...  19.9 us
    reduce_scatter x1, waiting for transfers between devices, shards(): total = lax.psum_scatter(flat, 'dp', scatter_dimension=0, tiled=True)[0]  15.9 us
    ppermute x1, waiting for transfers between devices, shards(): ahead = lax.ppermute(packed, 'expert', down_by)  11.1 us
    ppermute x1, starting transfers between devices, shards(): behind = lax.ppermute(packed, 'expert', up_by)  7.27 us
    pallas_call x1, Pallas kernels, shards(): pl.pallas_call(expert_kernel, out_shape=(bf16((replicas, 3 * units * shar...  5.48 us
    ppermute x1, starting transfers between devices, shards(): peer = lax.ppermute(own, 'cuts', swap)  4 us
  transfers between devices with their start and end apart: 6, of which 4 were waited for; matrix products, arithmetic and copies ran while one was open for 0% of the time, Pallas kernels for 1%

profile of v3, /device:TPU:1, one launch (start us, length us, event | category | flops | bytes accessed | tf_op | source)
XLA Modules:
  0.0 170.1 jit_solution(6441128180052727582)
XLA Ops:
  7.2 0.0 reduce-scatter.2.cloned.1.call-start
  7.2 1.6 pack.1.own
  8.8 19.9 %collective-permute-start.2 = (bf16[24,2176]{1,0:T(8,128)(2,1)}, bf16[24,2176]{1,0:T(8,128)(2,1)S(1)}, u32[]{:S(2)}, u32[]{:S(2)}) collective-permute-start(bf16[24,2176]{1,0:T(8,128)(2,1)} %pack.1.own), channel_id=1, source_target_pairs={{0,512},{16,528},{32,544},{48,560},{64,576},{80,592},{96,608},{112... | collective-permute-start | bytes 313352 | tf_op jit(solution)/shard_map/ppermute | solution.py:244
  28.7 1.9 %collective-permute-start.1 = (bf16[24,2176]{1,0:T(8,128)(2,1)}, bf16[24,2176]{1,0:T(8,128)(2,1)S(1)}, u32[]{:S(2)}, u32[]{:S(2)}) collective-permute-start(bf16[24,2176]{1,0:T(8,128)(2,1)} %pack.1.own), channel_id=1, source_target_pairs={{256,0},{272,16},{288,32},{304,48},{320,64},{336,80},{352,96},{368... | collective-permute-start | bytes 313352 | tf_op jit(solution)/shard_map/ppermute | solution.py:243
  30.7 7.3 %collective-permute-start = (bf16[24,2176]{1,0:T(8,128)(2,1)}, bf16[24,2176]{1,0:T(8,128)(2,1)S(1)}, u32[]{:S(2)}, u32[]{:S(2)}) collective-permute-start(bf16[24,2176]{1,0:T(8,128)(2,1)} %pack.1.own), channel_id=1, source_target_pairs={{0,256},{16,272},{32,288},{48,304},{64,320},{80,336},{96,352},{112... | collective-permute-start | bytes 313352 | tf_op jit(solution)/shard_map/ppermute | solution.py:242
  38.0 0.1 pad_add_fusion.place
  38.0 0.0 collective-permute-done.2.across
  38.0 11.1 %collective-permute-done.1.ahead = bf16[24,2176]{1,0:T(8,128)(2,1)S(1)} collective-permute-done((bf16[24,2176]{1,0:T(8,128)(2,1)}, bf16[24,2176]{1,0:T(8,128)(2,1)S(1)}, u32[]{:S(2)}, u32[]{:S(2)}) %collective-permute-start.1) | collective-permute-done | bytes 104480 | tf_op jit(solution)/shard_map/ppermute | solution.py:243
  49.2 0.0 collective-permute-done.behind
  49.2 0.9 copy-done.3
  50.1 2.1 %pick.1 = bf16[256,2048]{1,0:T(8,128)(2,1)S(1)} custom-call(s32[2]{0:T(128)S(1)} %pad_add_fusion.place, bf16[24,2176]{1,0:T(8,128)(2,1)S(1)} %copy-done.3, bf16[24,2176]{1,0:T(8,128)(2,1)S(1)} %collective-permute-done.behind, bf16[24,2176]{1,0:T(8,128)(2,1)S(1)} %collective-permute-done.1.ahead, bf16[24,2176]{1,0:T(8,128)(2,1)S(1)} %collective-permute-done.2.across), custom_call_target="tpu_custom_call" | custom-call | tf_op jit(solution)/shard_map/pick/pallas_call | solution.py:245
  52.1 30.9 %all_to_all.10 = bf16[16,16,2048]{2,1,0:T(8,128)(2,1)S(1)} all-to-all(bf16[16,16,2048]{2,1,0:T(8,128)(2,1)S(1)} %bitcast.19), channel_id=1, replica_groups={{0,16,32,48,64,80,96,112,128,144,160,176,192,208,224,240},{256,272,288,..., dimensions={0} | all-to-all | bytes 2097152 | tf_op jit(solution)/shard_map/all_to_all | solution.py:254
  83.0 4.0 %collective-permute-start.3 = (bf16[256,2048]{1,0:T(8,128)(2,1)S(1)}, bf16[256,2048]{1,0:T(8,128)(2,1)S(1)}, u32[]{:S(2)}, u32[]{:S(2)}) collective-permute-start(bf16[256,2048]{1,0:T(8,128)(2,1)S(1)} %bitcast.20), channel_id=1, source_target_pairs={{0,8},{8,0},{1,9},{9,1},{2,10},{10,2},{3,11},{11,3},{4,12},{12,4},... | collective-permute-start | bytes 3145736 | tf_op jit(solution)/shard_map/ppermute | solution.py:258
  87.1 2.3 %collective-permute-done.3.peer = bf16[256,2048]{1,0:T(8,128)(2,1)S(1)} collective-permute-done((bf16[256,2048]{1,0:T(8,128)(2,1)S(1)}, bf16[256,2048]{1,0:T(8,128)(2,1)S(1)}, u32[]{:S(2)}, u32[]{:S(2)}) %collective-permute-start.3) | collective-permute-done | bytes 1048608 | tf_op jit(solution)/shard_map/ppermute | solution.py:258
  89.3 0.0 copy-done
  89.3 0.0 copy-done.1
  89.3 5.5 %expert.1 = (bf16[8,2304,128]{2,1,0:T(8,128)(2,1)}, bf16[256,768]{1,0:T(8,128)(2,1)S(1)}) custom-call(s32[1]{0:T(128)} %bitcast.1.cut.place, bf16[256,2048]{1,0:T(8,128)(2,1)S(1)} %bitcast.21, bf16[256,2048]{1,0:T(8,128)(2,1)S(1)} %collective-permute-done.3.peer, bf16[2048,384]{1,0:T(8,128)(2,1)S(1)} %bitcast.15, bf16[2048,384]{1,0:T(8,128)(2,1)S(1)} %bitcast.17, ...), custom_call_target="tpu_custom_call" | custom-call | tf_op jit(solution)/shard_map/expert/pallas_call | solution.py:260
  94.8 0.0 reduce-scatter.2.cloned.1.call-update
  94.8 1.3 rows.1
  96.1 2.3 %collective-permute-start.4 = (bf16[256,1024]{1,0:T(8,128)(2,1)S(1)}, bf16[256,1024]{1,0:T(8,128)(2,1)S(1)}, u32[]{:S(2)}, u32[]{:S(2)}) collective-permute-start(bf16[256,1024]{1,0:T(8,128)(2,1)S(1)} %get-tuple-element.13), channel_id=1, source_target_pairs={{0,8},{8,0},{1,9},{9,1},{2,10},{10,2},{3,11},{11,3},{4,12},{12,4},... | collective-permute-start | bytes 1572872 | tf_op jit(solution)/shard_map/ppermute | solution.py:288
  98.4 1.5 collective-permute-done.4
  99.9 0.1 add_convert_fusion
  100.1 0.2 reshape.29
  100.3 0.0 copy-start.4
  100.3 0.2 copy.11
  100.5 43.6 %all_to_all.11 = bf16[64,4,1024]{2,1,0:T(4,128)(2,1)S(1)} all-to-all(bf16[64,4,1024]{2,1,0:T(4,128)(2,1)S(1)} %bitcast.26), channel_id=1, replica_groups=mesh['expert'=64,'cuts'=2,'dp'=8] {'expert'}, dimensions={0} | all-to-all | bytes 1048576 | tf_op jit(solution)/shard_map/all_to_all | solution.py:289
  144.1 0.1 reshape.31.returned
  144.2 0.0 copy-done.4
  144.2 1.2 combine.1
  145.4 15.9 %reduce-scatter.2.cloned.1.call-done = bf16[1,2304,128]{2,1,0:T(8,128)(2,1)} async-done(((bf16[8,2304,128]{2,1,0:T(8,128)(2,1)}), bf16[1,2304,128]{2,1,0:T(8,128)(2,1)}) %reduce-scatter.2.cloned.1.call-update) | async-done | bytes 589840 | tf_op jit(solution)/shard_map/reduce_scatter | solution.py:278
  161.3 1.1 copy-done.2
  162.3 1.0 unpack.1
  (4 shorter events, 0.0 us)
Async XLA Ops:
  7.2 154.1 %reduce-scatter.2.cloned.1.call-start = ((), (), s32[]{:S(2)}) async-start(), calls=%async_computation.3 | async-start | bytes 5308416 | tf_op jit(solution)/shard_map/reduce_scatter | solution.py:278
  8.8 29.2 %collective-permute-start.2 = (bf16[24,2176]{1,0:T(8,128)(2,1)}, bf16[24,2176]{1,0:T(8,128)(2,1)S(1)}, u32[]{:S(2)}, u32[]{:S(2)}) collective-permute-start(bf16[24,2176]{1,0:T(8,128)(2,1)} %pack.1.own), channel_id=1, source_target_pairs={{0,512},{16,528},{32,544},{48,560},{64,576},{80,592},{96,608},{112... | collective-permute-start | bytes 313352 | tf_op jit(solution)/shard_map/ppermute | solution.py:244
  28.7 20.4 %collective-permute-start.1 = (bf16[24,2176]{1,0:T(8,128)(2,1)}, bf16[24,2176]{1,0:T(8,128)(2,1)S(1)}, u32[]{:S(2)}, u32[]{:S(2)}) collective-permute-start(bf16[24,2176]{1,0:T(8,128)(2,1)} %pack.1.own), channel_id=1, source_target_pairs={{256,0},{272,16},{288,32},{304,48},{320,64},{336,80},{352,96},{368... | collective-permute-start | bytes 313352 | tf_op jit(solution)/shard_map/ppermute | solution.py:243
  30.7 18.5 %collective-permute-start = (bf16[24,2176]{1,0:T(8,128)(2,1)}, bf16[24,2176]{1,0:T(8,128)(2,1)S(1)}, u32[]{:S(2)}, u32[]{:S(2)}) collective-permute-start(bf16[24,2176]{1,0:T(8,128)(2,1)} %pack.1.own), channel_id=1, source_target_pairs={{0,256},{16,272},{32,288},{48,304},{64,320},{80,336},{96,352},{112... | collective-permute-start | bytes 313352 | tf_op jit(solution)/shard_map/ppermute | solution.py:242
  38.0 51.3 %copy-start = (bf16[2048,1,384]{2,0,1:T(8,128)(2,1)S(1)}, bf16[2048,1,384]{2,0,1:T(8,128)(2,1)}, u32[]{:S(2)}) copy-start(bf16[2048,1,384]{2,0,1:T(8,128)(2,1)} %param.11) | copy-start | bytes 4718596
  38.0 51.3 %copy-start.1 = (bf16[2048,1,384]{2,0,1:T(8,128)(2,1)S(1)}, bf16[2048,1,384]{2,0,1:T(8,128)(2,1)}, u32[]{:S(2)}) copy-start(bf16[2048,1,384]{2,0,1:T(8,128)(2,1)} %param.12) | copy-start | bytes 4718596
  49.2 0.9 copy-start.3
  83.0 6.3 %collective-permute-start.3 = (bf16[256,2048]{1,0:T(8,128)(2,1)S(1)}, bf16[256,2048]{1,0:T(8,128)(2,1)S(1)}, u32[]{:S(2)}, u32[]{:S(2)}) collective-permute-start(bf16[256,2048]{1,0:T(8,128)(2,1)S(1)} %bitcast.20), channel_id=1, source_target_pairs={{0,8},{8,0},{1,9},{9,1},{2,10},{10,2},{3,11},{11,3},{4,12},{12,4},... | collective-permute-start | bytes 3145736 | tf_op jit(solution)/shard_map/ppermute | solution.py:258
  96.1 3.8 %collective-permute-start.4 = (bf16[256,1024]{1,0:T(8,128)(2,1)S(1)}, bf16[256,1024]{1,0:T(8,128)(2,1)S(1)}, u32[]{:S(2)}, u32[]{:S(2)}) collective-permute-start(bf16[256,1024]{1,0:T(8,128)(2,1)S(1)} %get-tuple-element.13), channel_id=1, source_target_pairs={{0,8},{8,0},{1,9},{9,1},{2,10},{10,2},{3,11},{11,3},{4,12},{12,4},... | collective-permute-start | bytes 1572872 | tf_op jit(solution)/shard_map/ppermute | solution.py:288
  100.3 43.9 %copy-start.4 = (s32[24,8]{0,1:T(8,128)S(1)}, s32[24,8]{0,1:T(8,128)}, u32[]{:S(2)}) copy-start(s32[24,8]{0,1:T(8,128)} %param.9) | copy-start | bytes 2308
  161.2 1.1 copy-start.2
Sparse Core Ops, SparseCore 0:
  95.0 66.2 reduce-scatter.1

commit v4 on v3

--- a/solution.py
+++ b/solution.py
@@ -124,9 +124,11 @@
 
 
 def expert_kernel(
-    place, own, peer, gate_hbm, up_hbm, down_hbm, flat_hbm, backs,
+    place, own, peer, gate_hbm, up_hbm, down_hbm, flat_hbm, turned, backs,
     rows, grads, gate, up, down, flat, sems, out_sems,
 ):
+    me = place[1]
+
     def copies(rows_from, grads_from):
         pairs = ((rows_from, rows), (gate_hbm, gate), (up_hbm, up), (grads_from, grads), (down_hbm, down))
         return [pltpu.make_async_copy(a, b, sems.at[i]) for i, (a, b) in enumerate(pairs)]
@@ -165,9 +167,10 @@
         part = dot(hidden_t, grads[:, columns], 1, 0).astype(jnp.bfloat16)
         for h in range(per):
             lanes = slice(h * 128, (h + 1) * 128)
-            start = 2 * per * units + (i * per + h) * strip
+            start = (i * per + h) * strip
             for j in range(replicas):
-                flat[j, start : start + strip, :] = part[j * strip : (j + 1) * strip, lanes]
+                ahead = jnp.bitwise_and(j - me + replicas, replicas - 1)
+                turned[ahead, start : start + strip, :] = part[j * strip : (j + 1) * strip, lanes]
     both = jnp.concatenate((back_hid * up_val * slope, back_hid * activated), axis=1)
     backs[...] = both.astype(jnp.bfloat16)
     both_t = both.T.astype(jnp.bfloat16)
@@ -196,7 +199,7 @@
     mine[...] = part(cut[0])
 
 
-def unpack_kernel(total, gate, up, down):
+def unpack_kernel(total, down_total, gate, up, down):
     units = gate.shape[1]
     per = gate.shape[0] // 128
     strip = down.shape[0]
@@ -205,9 +208,34 @@
         lanes = slice(h * 128, (h + 1) * 128)
         gate[lanes, :] = total[at : at + units, :].astype(jnp.float32).T.astype(jnp.bfloat16)
         up[lanes, :] = total[at + units : at + 2 * units, :].astype(jnp.float32).T.astype(jnp.bfloat16)
-    base = per * 2 * units
     for j in range(down.shape[1] // 128):
-        down[:, j * 128 : (j + 1) * 128] = total[base + j * strip : base + (j + 1) * strip, :]
+        down[:, j * 128 : (j + 1) * 128] = down_total[j * strip : (j + 1) * strip, :]
+
+
+def ring_sum(turned):
+    size = turned.shape[0]
+    half = turned.shape[1] // 2
+    onward = [(i, (i + 1) % size) for i in range(size)]
+    back = [(j, i) for i, j in onward]
+
+    def add(a, b):
+        return (a.astype(jnp.float32) + b.astype(jnp.float32)).astype(jnp.bfloat16)
+
+    far = turned[size // 2]
+    right = lax.ppermute(far[:half], "dp", onward)
+    left = lax.ppermute(far[half:], "dp", back)
+    for step in range(size // 2 - 1, 0, -1):
+        r, l = turned[step], turned[size - step]
+        if step == size // 2 - 1:
+            right = jnp.concatenate((add(right, r[:half]), r[half:]), axis=0)
+            left = jnp.concatenate((l[:half], add(left, l[half:])), axis=0)
+        else:
+            right, left = add(right, r), add(left, l)
+        right = lax.ppermute(right, "dp", onward)
+        left = lax.ppermute(left, "dp", back)
+    return (
+        turned[0].astype(jnp.float32) + right.astype(jnp.float32) + left.astype(jnp.float32)
+    ).astype(jnp.bfloat16)
 
 
 def shards(tokens, out_grad, expert_ids, route_probs, gate_weight, up_weight, down_weight):
@@ -257,24 +285,32 @@
     ).reshape(SLOTS, width)
     peer = lax.ppermute(own, "cuts", swap)
 
-    flat, backs = pl.pallas_call(
+    flat, turned, backs = pl.pallas_call(
         expert_kernel,
-        out_shape=(bf16((replicas, 3 * units * share // 128, 128)), bf16((SLOTS, 2 * units))),
+        out_shape=(
+            bf16((replicas, 2 * units * share // 128, 128)),
+            bf16((replicas, strip * width // 128, 128)),
+            bf16((SLOTS, 2 * units)),
+        ),
         in_specs=[SMEM, HBM] + [ANY] * 4,
-        out_specs=(HBM, VMEM),
+        out_specs=(HBM, VMEM, VMEM),
         scratch_shapes=[
             pltpu.VMEM((SLOTS, width), jnp.bfloat16),
             pltpu.VMEM((SLOTS, width), jnp.bfloat16),
             pltpu.VMEM((width, units), jnp.bfloat16),
             pltpu.VMEM((width, units), jnp.bfloat16),
             pltpu.VMEM((units, width), jnp.bfloat16),
-            pltpu.VMEM((replicas, 3 * units * share // 128, 128), jnp.bfloat16),
+            pltpu.VMEM((replicas, 2 * units * share // 128, 128), jnp.bfloat16),
             pltpu.SemaphoreType.DMA((5,)),
             pltpu.SemaphoreType.DMA((replicas,)),
         ],
-        compiler_params=pltpu.CompilerParams(vmem_limit_bytes=48 * 1024 * 1024),
+        compiler_params=pltpu.CompilerParams(vmem_limit_bytes=46 * 1024 * 1024),
         name="expert",
-    )(cut, own, peer, w_gate, w_up, w_down)
+    )(
+        jnp.stack((lax.axis_index("cuts"), lax.axis_index("dp"))).astype(jnp.int32),
+        own, peer, w_gate, w_up, w_down,
+    )
+    down_total = ring_sum(turned)
     total = lax.psum_scatter(flat, "dp", scatter_dimension=0, tiled=True)[0]
 
     mine, other = pl.pallas_call(
@@ -303,11 +339,11 @@
     gate_grad, up_grad, down_grad = pl.pallas_call(
         unpack_kernel,
         out_shape=(bf16((share, units)), bf16((share, units)), bf16((strip, width))),
-        in_specs=[VMEM],
+        in_specs=[VMEM] * 2,
         out_specs=(VMEM,) * 3,
         compiler_params=PARAMS,
         name="unpack",
-    )(total)
+    )(total, down_total)
     return (result, gate_grad[:, None, :], up_grad[:, None, :], down_grad[:, None, :])
 
 

time: 171 us -> 183 us (1.070)
  the two profiles are of different devices: /device:TPU:1 before, /device:TPU:16 now
where the time goes in v4:
time: 183 us; the launch traced here: 182 us
  starting transfers between devices  73.4 us (40%)
  waiting for transfers between devices  43.4 us (24%)
  blocking collectives  33.2 us (18%)
  between operations  14.3 us (8%)
  Pallas kernels  12.9 us (7%)
  local copies, waits for them, and re-layouts  4.43 us (2%)
    all_to_all x1, blocking collectives, shards(): lax.all_to_all(sent.reshape(16, 4 * CAP, width), 'expert', split_axis=0,...  33.2 us
    ppermute x1, starting transfers between devices, shards(): lax.ppermute(packed, 'expert', [(i, (i + 32) % EXPERTS) for i in range(EX...  19.4 us
    ppermute x3, waiting for transfers between devices, ring_sum(): left = lax.ppermute(left, 'dp', back)  15.7 us
    ppermute x3, starting transfers between devices, ring_sum(): right = lax.ppermute(right, 'dp', onward)  15.6 us
    all_to_all x1, starting transfers between devices, shards(): lax.all_to_all(mine.astype(jnp.bfloat16).reshape(16, 4, CAP, half).transp...  13.1 us
    ppermute x1, waiting for transfers between devices, shards(): ahead = lax.ppermute(packed, 'expert', down_by)  10.1 us
    ppermute x1, starting transfers between devices, shards(): behind = lax.ppermute(packed, 'expert', up_by)  7.83 us
    pallas_call x1, Pallas kernels, shards(): pl.pallas_call(expert_kernel, out_shape=(bf16((replicas, 2 * units * shar...  6.4 us
  transfers between devices with their start and end apart: 15, of which 11 were waited for; matrix products, arithmetic and copies ran while one was open for 1% of the time, Pallas kernels for 1%

profile of v4, /device:TPU:16, one launch (start us, length us, event | category | flops | bytes accessed | tf_op | source)
XLA Modules:
  0.0 182.3 jit_solution(12289252678339563089)
XLA Ops:
  7.2 1.6 pack.1.own
  8.8 19.4 %collective-permute-start.2 = (bf16[24,2176]{1,0:T(8,128)(2,1)}, bf16[24,2176]{1,0:T(8,128)(2,1)S(1)}, u32[]{:S(2)}, u32[]{:S(2)}) collective-permute-start(bf16[24,2176]{1,0:T(8,128)(2,1)} %pack.1.own), channel_id=1, source_target_pairs={{0,512},{16,528},{32,544},{48,560},{64,576},{80,592},{96,608},{112... | collective-permute-start | bytes 313352 | tf_op jit(solution)/shard_map/ppermute | solution.py:272
  28.2 1.9 %collective-permute-start.1 = (bf16[24,2176]{1,0:T(8,128)(2,1)}, bf16[24,2176]{1,0:T(8,128)(2,1)S(1)}, u32[]{:S(2)}, u32[]{:S(2)}) collective-permute-start(bf16[24,2176]{1,0:T(8,128)(2,1)} %pack.1.own), channel_id=1, source_target_pairs={{256,0},{272,16},{288,32},{304,48},{320,64},{336,80},{352,96},{368... | collective-permute-start | bytes 313352 | tf_op jit(solution)/shard_map/ppermute | solution.py:271
  30.1 7.8 %collective-permute-start = (bf16[24,2176]{1,0:T(8,128)(2,1)}, bf16[24,2176]{1,0:T(8,128)(2,1)S(1)}, u32[]{:S(2)}, u32[]{:S(2)}) collective-permute-start(bf16[24,2176]{1,0:T(8,128)(2,1)} %pack.1.own), channel_id=1, source_target_pairs={{0,256},{16,272},{32,288},{48,304},{64,320},{80,336},{96,352},{112... | collective-permute-start | bytes 313352 | tf_op jit(solution)/shard_map/ppermute | solution.py:270
  38.1 10.1 %collective-permute-done.1.ahead = bf16[24,2176]{1,0:T(8,128)(2,1)S(1)} collective-permute-done((bf16[24,2176]{1,0:T(8,128)(2,1)}, bf16[24,2176]{1,0:T(8,128)(2,1)S(1)}, u32[]{:S(2)}, u32[]{:S(2)}) %collective-permute-start.1) | collective-permute-done | bytes 104480 | tf_op jit(solution)/shard_map/ppermute | solution.py:271
  49.1 1.5 pick.1
  50.6 33.2 %all_to_all.10 = bf16[16,16,2048]{2,1,0:T(8,128)(2,1)} all-to-all(bf16[16,16,2048]{2,1,0:T(8,128)(2,1)S(1)} %bitcast.49), channel_id=1, replica_groups={{0,16,32,48,64,80,96,112,128,144,160,176,192,208,224,240},{256,272,288,..., dimensions={0} | all-to-all | bytes 2097152 | tf_op jit(solution)/shard_map/all_to_all | solution.py:282
  83.8 1.9 %collective-permute-start.3 = (bf16[256,2048]{1,0:T(8,128)(2,1)}, bf16[256,2048]{1,0:T(8,128)(2,1)}, u32[]{:S(2)}, u32[]{:S(2)}) collective-permute-start(bf16[256,2048]{1,0:T(8,128)(2,1)} %bitcast.6.own), channel_id=1, source_target_pairs={{0,8},{8,0},{1,9},{9,1},{2,10},{10,2},{3,11},{11,3},{4,12},{12,4},... | collective-permute-start | bytes 3145736 | tf_op jit(solution)/shard_map/ppermute | solution.py:286
  85.8 2.9 %collective-permute-done.3.peer = bf16[256,2048]{1,0:T(8,128)(2,1)} collective-permute-done((bf16[256,2048]{1,0:T(8,128)(2,1)}, bf16[256,2048]{1,0:T(8,128)(2,1)}, u32[]{:S(2)}, u32[]{:S(2)}) %collective-permute-start.3) | collective-permute-done | bytes 1048608 | tf_op jit(solution)/shard_map/ppermute | solution.py:286
  88.6 6.4 %expert.1 = (bf16[8,1536,128]{2,1,0:T(8,128)(2,1)}, bf16[8,768,128]{2,1,0:T(8,128)(2,1)S(1)}, bf16[256,768]{1,0:T(8,128)(2,1)S(1)}) custom-call(s32[2]{0:T(128)S(1)} %pad_add_fusion.place, bf16[256,2048]{1,0:T(8,128)(2,1)} %bitcast.6.own, bf16[256,2048]{1,0:T(8,128)(2,1)} %collective-permute-done.3.peer, bf16[2048,384]{1,0:T(8,128)(2,1)S(1)} %bitcast.45, ...), custom_call_target="tpu_custom_call" | custom-call | tf_op jit(solution)/shard_map/expert/pallas_call | solution.py:288
  95.1 1.2 copy-done.2
  96.3 1.3 rows.1
  97.5 2.1 %collective-permute-start.4 = (bf16[256,1024]{1,0:T(8,128)(2,1)S(1)}, bf16[256,1024]{1,0:T(8,128)(2,1)S(1)}, u32[]{:S(2)}, u32[]{:S(2)}) collective-permute-start(bf16[256,1024]{1,0:T(8,128)(2,1)S(1)} %get-tuple-element.14), channel_id=1, source_target_pairs={{0,8},{8,0},{1,9},{9,1},{2,10},{10,2},{3,11},{11,3},{4,12},{12,4},... | collective-permute-start | bytes 1572872 | tf_op jit(solution)/shard_map/ppermute | solution.py:324
  99.6 1.7 collective-permute-done.4
  101.7 1.0 copy.11
  102.7 13.1 %all-to-all-start.1 = ((bf16[64,4,1024]{2,1,0:T(4,128)(2,1)}), bf16[64,4,1024]{2,1,0:T(4,128)(2,1)S(1)}, u32[]{:S(2)}, u32[]{:S(2)}) async-start(bf16[64,4,1024]{2,1,0:T(4,128)(2,1)} %bitcast.11), calls=%async_computation.1 | async-start | bytes 1048576 | tf_op jit(solution)/shard_map/all_to_all | solution.py:325
  115.8 3.5 %collective-permute-start.5 = (bf16[384,128]{1,0:T(8,128)(2,1)S(1)}, bf16[384,128]{1,0:T(8,128)(2,1)S(1)}, u32[]{:S(2)}, u32[]{:S(2)}) collective-permute-start(bf16[384,128]{1,0:T(8,128)(2,1)S(1)} %get-tuple-element.26), channel_id=1, source_target_pairs={{0,1},{1,2},{2,3},{3,4},{4,5},{5,6},{6,7},{7,0},{8,9},{9,10},{10,1... | collective-permute-start | bytes 294920 | tf_op jit(solution)/shard_map/ppermute | solution.py:225
  119.3 2.4 %collective-permute-start.9 = (bf16[384,128]{1,0:T(8,128)(2,1)S(1)}, bf16[384,128]{1,0:T(8,128)(2,1)S(1)}, u32[]{:S(2)}, u32[]{:S(2)}) collective-permute-start(bf16[384,128]{1,0:T(8,128)(2,1)S(1)} %get-tuple-element.27), channel_id=1, source_target_pairs={{1,0},{2,1},{3,2},{4,3},{5,4},{6,5},{7,6},{0,7},{9,8},{10,9},{11,1... | collective-permute-start | bytes 294920 | tf_op jit(solution)/shard_map/ppermute | solution.py:226
  121.7 3.1 %collective-permute-done.5 = bf16[384,128]{1,0:T(8,128)(2,1)S(1)} collective-permute-done((bf16[384,128]{1,0:T(8,128)(2,1)S(1)}, bf16[384,128]{1,0:T(8,128)(2,1)S(1)}, u32[]{:S(2)}, u32[]{:S(2)}) %collective-permute-start.5) | collective-permute-done | bytes 98336 | tf_op jit(solution)/shard_map/ppermute | solution.py:225
  124.8 4.6 %collective-permute-done.9 = bf16[384,128]{1,0:T(8,128)(2,1)S(1)} collective-permute-done((bf16[384,128]{1,0:T(8,128)(2,1)S(1)}, bf16[384,128]{1,0:T(8,128)(2,1)S(1)}, u32[]{:S(2)}, u32[]{:S(2)}) %collective-permute-start.9) | collective-permute-done | bytes 98336 | tf_op jit(solution)/shard_map/ppermute | solution.py:226
  129.4 1.9 %collective-permute-start.10 = (bf16[768,128]{1,0:T(8,128)(2,1)S(1)}, bf16[768,128]{1,0:T(8,128)(2,1)S(1)}, u32[]{:S(2)}, u32[]{:S(2)}) collective-permute-start(bf16[768,128]{1,0:T(8,128)(2,1)S(1)} %pad_maximum_fusion.1), channel_id=1, source_target_pairs={{1,0},{2,1},{3,2},{4,3},{5,4},{6,5},{7,6},{0,7},{9,8},{10,9},{11,1... | collective-permute-start | bytes 589832 | tf_op jit(solution)/shard_map/ppermute | solution.py:235
  131.4 4.8 %collective-permute-start.6 = (bf16[768,128]{1,0:T(8,128)(2,1)S(1)}, bf16[768,128]{1,0:T(8,128)(2,1)S(1)}, u32[]{:S(2)}, u32[]{:S(2)}) collective-permute-start(bf16[768,128]{1,0:T(8,128)(2,1)S(1)} %pad_maximum_fusion), channel_id=1, source_target_pairs={{0,1},{1,2},{2,3},{3,4},{4,5},{5,6},{6,7},{7,0},{8,9},{9,10},{10,1... | collective-permute-start | bytes 589832 | tf_op jit(solution)/shard_map/ppermute | solution.py:234
  136.2 7.5 %collective-permute-done.10 = bf16[768,128]{1,0:T(8,128)(2,1)S(1)} collective-permute-done((bf16[768,128]{1,0:T(8,128)(2,1)S(1)}, bf16[768,128]{1,0:T(8,128)(2,1)S(1)}, u32[]{:S(2)}, u32[]{:S(2)}) %collective-permute-start.10) | collective-permute-done | bytes 196640 | tf_op jit(solution)/shard_map/ppermute | solution.py:235
  144.3 5.7 %collective-permute-start.7 = (bf16[768,128]{1,0:T(8,128)(2,1)S(1)}, bf16[768,128]{1,0:T(8,128)(2,1)S(1)}, u32[]{:S(2)}, u32[]{:S(2)}) collective-permute-start(bf16[768,128]{1,0:T(8,128)(2,1)S(1)} %get-tuple-element.22), channel_id=1, source_target_pairs={{0,1},{1,2},{2,3},{3,4},{4,5},{5,6},{6,7},{7,0},{8,9},{9,10},{10,1... | collective-permute-start | bytes 589832 | tf_op jit(solution)/shard_map/ppermute | solution.py:234
  150.0 1.9 %collective-permute-start.11 = (bf16[768,128]{1,0:T(8,128)(2,1)S(1)}, bf16[768,128]{1,0:T(8,128)(2,1)S(1)}, u32[]{:S(2)}, u32[]{:S(2)}) collective-permute-start(bf16[768,128]{1,0:T(8,128)(2,1)S(1)} %get-tuple-element.23), channel_id=1, source_target_pairs={{1,0},{2,1},{3,2},{4,3},{5,4},{6,5},{7,6},{0,7},{9,8},{10,9},{11,1... | collective-permute-start | bytes 589832 | tf_op jit(solution)/shard_map/ppermute | solution.py:235
  151.9 3.5 %collective-permute-done.7 = bf16[768,128]{1,0:T(8,128)(2,1)S(1)} collective-permute-done((bf16[768,128]{1,0:T(8,128)(2,1)S(1)}, bf16[768,128]{1,0:T(8,128)(2,1)S(1)}, u32[]{:S(2)}, u32[]{:S(2)}) %collective-permute-start.7) | collective-permute-done | bytes 196640 | tf_op jit(solution)/shard_map/ppermute | solution.py:234
  155.4 3.8 %collective-permute-done.11 = bf16[768,128]{1,0:T(8,128)(2,1)S(1)} collective-permute-done((bf16[768,128]{1,0:T(8,128)(2,1)S(1)}, bf16[768,128]{1,0:T(8,128)(2,1)S(1)}, u32[]{:S(2)}, u32[]{:S(2)}) %collective-permute-start.11) | collective-permute-done | bytes 196640 | tf_op jit(solution)/shard_map/ppermute | solution.py:235
  159.4 5.1 %collective-permute-start.8 = (bf16[768,128]{1,0:T(8,128)(2,1)S(1)}, bf16[768,128]{1,0:T(8,128)(2,1)S(1)}, u32[]{:S(2)}, u32[]{:S(2)}) collective-permute-start(bf16[768,128]{1,0:T(8,128)(2,1)S(1)} %get-tuple-element.20), channel_id=1, source_target_pairs={{0,1},{1,2},{2,3},{3,4},{4,5},{5,6},{6,7},{7,0},{8,9},{9,10},{10,1... | collective-permute-start | bytes 589832 | tf_op jit(solution)/shard_map/ppermute | solution.py:234
  164.5 1.9 %collective-permute-start.12 = (bf16[768,128]{1,0:T(8,128)(2,1)S(1)}, bf16[768,128]{1,0:T(8,128)(2,1)S(1)}, u32[]{:S(2)}, u32[]{:S(2)}) collective-permute-start(bf16[768,128]{1,0:T(8,128)(2,1)S(1)} %get-tuple-element.21), channel_id=1, source_target_pairs={{1,0},{2,1},{3,2},{4,3},{5,4},{6,5},{7,6},{0,7},{9,8},{10,9},{11,1... | collective-permute-start | bytes 589832 | tf_op jit(solution)/shard_map/ppermute | solution.py:235
  166.4 1.2 collective-permute-done.8
  167.7 4.4 %collective-permute-done.12 = bf16[768,128]{1,0:T(8,128)(2,1)S(1)} collective-permute-done((bf16[768,128]{1,0:T(8,128)(2,1)S(1)}, bf16[768,128]{1,0:T(8,128)(2,1)S(1)}, u32[]{:S(2)}, u32[]{:S(2)}) %collective-permute-start.12) | collective-permute-done | bytes 196640 | tf_op jit(solution)/shard_map/ppermute | solution.py:235
  172.3 1.2 combine.1
  (33 shorter events, 4.5 us)
Async XLA Ops:
  7.2 166.3 %reduce-scatter.2.cloned.1.call-start = ((), (), s32[]{:S(2)}) async-start(), calls=%async_computation.3 | async-start | bytes 3538944 | tf_op jit(solution)/shard_map/reduce_scatter | solution.py:314
  8.8 29.2 %collective-permute-start.2 = (bf16[24,2176]{1,0:T(8,128)(2,1)}, bf16[24,2176]{1,0:T(8,128)(2,1)S(1)}, u32[]{:S(2)}, u32[]{:S(2)}) collective-permute-start(bf16[24,2176]{1,0:T(8,128)(2,1)} %pack.1.own), channel_id=1, source_target_pairs={{0,512},{16,528},{32,544},{48,560},{64,576},{80,592},{96,608},{112... | collective-permute-start | bytes 313352 | tf_op jit(solution)/shard_map/ppermute | solution.py:272
  28.2 20.0 %collective-permute-start.1 = (bf16[24,2176]{1,0:T(8,128)(2,1)}, bf16[24,2176]{1,0:T(8,128)(2,1)S(1)}, u32[]{:S(2)}, u32[]{:S(2)}) collective-permute-start(bf16[24,2176]{1,0:T(8,128)(2,1)} %pack.1.own), channel_id=1, source_target_pairs={{256,0},{272,16},{288,32},{304,48},{320,64},{336,80},{352,96},{368... | collective-permute-start | bytes 313352 | tf_op jit(solution)/shard_map/ppermute | solution.py:271
  30.1 18.1 %collective-permute-start = (bf16[24,2176]{1,0:T(8,128)(2,1)}, bf16[24,2176]{1,0:T(8,128)(2,1)S(1)}, u32[]{:S(2)}, u32[]{:S(2)}) collective-permute-start(bf16[24,2176]{1,0:T(8,128)(2,1)} %pack.1.own), channel_id=1, source_target_pairs={{0,256},{16,272},{32,288},{48,304},{64,320},{80,336},{96,352},{112... | collective-permute-start | bytes 313352 | tf_op jit(solution)/shard_map/ppermute | solution.py:270
  38.0 50.6 %copy-start = (bf16[2048,1,384]{2,0,1:T(8,128)(2,1)S(1)}, bf16[2048,1,384]{2,0,1:T(8,128)(2,1)}, u32[]{:S(2)}) copy-start(bf16[2048,1,384]{2,0,1:T(8,128)(2,1)} %param.11) | copy-start | bytes 4718596
  38.0 50.6 %copy-start.1 = (bf16[2048,1,384]{2,0,1:T(8,128)(2,1)S(1)}, bf16[2048,1,384]{2,0,1:T(8,128)(2,1)}, u32[]{:S(2)}) copy-start(bf16[2048,1,384]{2,0,1:T(8,128)(2,1)} %param.12) | copy-start | bytes 4718596
  48.2 0.9 copy-start.4
  83.8 4.9 %collective-permute-start.3 = (bf16[256,2048]{1,0:T(8,128)(2,1)}, bf16[256,2048]{1,0:T(8,128)(2,1)}, u32[]{:S(2)}, u32[]{:S(2)}) collective-permute-start(bf16[256,2048]{1,0:T(8,128)(2,1)} %bitcast.6.own), channel_id=1, source_target_pairs={{0,8},{8,0},{1,9},{9,1},{2,10},{10,2},{3,11},{11,3},{4,12},{12,4},... | collective-permute-start | bytes 3145736 | tf_op jit(solution)/shard_map/ppermute | solution.py:286
  95.1 1.2 copy-start.2
  97.5 3.8 %collective-permute-start.4 = (bf16[256,1024]{1,0:T(8,128)(2,1)S(1)}, bf16[256,1024]{1,0:T(8,128)(2,1)S(1)}, u32[]{:S(2)}, u32[]{:S(2)}) collective-permute-start(bf16[256,1024]{1,0:T(8,128)(2,1)S(1)} %get-tuple-element.14), channel_id=1, source_target_pairs={{0,8},{8,0},{1,9},{9,1},{2,10},{10,2},{3,11},{11,3},{4,12},{12,4},... | collective-permute-start | bytes 1572872 | tf_op jit(solution)/shard_map/ppermute | solution.py:324
  101.5 14.3 %copy-start.3 = (bf16[8,768,128]{2,1,0:T(8,128)(2,1)S(1)}, bf16[8,768,128]{2,1,0:T(8,128)(2,1)}, u32[]{:S(2)}) copy-start(bf16[8,768,128]{2,1,0:T(8,128)(2,1)} %copy-done.2) | copy-start | bytes 4718596
  102.7 69.4 %all-to-all-start.1 = ((bf16[64,4,1024]{2,1,0:T(4,128)(2,1)}), bf16[64,4,1024]{2,1,0:T(4,128)(2,1)S(1)}, u32[]{:S(2)}, u32[]{:S(2)}) async-start(bf16[64,4,1024]{2,1,0:T(4,128)(2,1)} %bitcast.11), calls=%async_computation.1 | async-start | bytes 1048576 | tf_op jit(solution)/shard_map/all_to_all | solution.py:325
  115.8 9.0 %collective-permute-start.5 = (bf16[384,128]{1,0:T(8,128)(2,1)S(1)}, bf16[384,128]{1,0:T(8,128)(2,1)S(1)}, u32[]{:S(2)}, u32[]{:S(2)}) collective-permute-start(bf16[384,128]{1,0:T(8,128)(2,1)S(1)} %get-tuple-element.26), channel_id=1, source_target_pairs={{0,1},{1,2},{2,3},{3,4},{4,5},{5,6},{6,7},{7,0},{8,9},{9,10},{10,1... | collective-permute-start | bytes 294920 | tf_op jit(solution)/shard_map/ppermute | solution.py:225
  119.3 10.0 %collective-permute-start.9 = (bf16[384,128]{1,0:T(8,128)(2,1)S(1)}, bf16[384,128]{1,0:T(8,128)(2,1)S(1)}, u32[]{:S(2)}, u32[]{:S(2)}) collective-permute-start(bf16[384,128]{1,0:T(8,128)(2,1)S(1)} %get-tuple-element.27), channel_id=1, source_target_pairs={{1,0},{2,1},{3,2},{4,3},{5,4},{6,5},{7,6},{0,7},{9,8},{10,9},{11,1... | collective-permute-start | bytes 294920 | tf_op jit(solution)/shard_map/ppermute | solution.py:226
  129.4 14.2 %collective-permute-start.10 = (bf16[768,128]{1,0:T(8,128)(2,1)S(1)}, bf16[768,128]{1,0:T(8,128)(2,1)S(1)}, u32[]{:S(2)}, u32[]{:S(2)}) collective-permute-start(bf16[768,128]{1,0:T(8,128)(2,1)S(1)} %pad_maximum_fusion.1), channel_id=1, source_target_pairs={{1,0},{2,1},{3,2},{4,3},{5,4},{6,5},{7,6},{0,7},{9,8},{10,9},{11,1... | collective-permute-start | bytes 589832 | tf_op jit(solution)/shard_map/ppermute | solution.py:235
  131.4 12.8 %collective-permute-start.6 = (bf16[768,128]{1,0:T(8,128)(2,1)S(1)}, bf16[768,128]{1,0:T(8,128)(2,1)S(1)}, u32[]{:S(2)}, u32[]{:S(2)}) collective-permute-start(bf16[768,128]{1,0:T(8,128)(2,1)S(1)} %pad_maximum_fusion), channel_id=1, source_target_pairs={{0,1},{1,2},{2,3},{3,4},{4,5},{5,6},{6,7},{7,0},{8,9},{9,10},{10,1... | collective-permute-start | bytes 589832 | tf_op jit(solution)/shard_map/ppermute | solution.py:234
  144.3 28.0 %copy-start.6 = (s32[24,8]{0,1:T(8,128)S(1)}, s32[24,8]{0,1:T(8,128)}, u32[]{:S(2)}) copy-start(s32[24,8]{0,1:T(8,128)} %param.9) | copy-start | bytes 2308
  144.3 11.1 %collective-permute-start.7 = (bf16[768,128]{1,0:T(8,128)(2,1)S(1)}, bf16[768,128]{1,0:T(8,128)(2,1)S(1)}, u32[]{:S(2)}, u32[]{:S(2)}) collective-permute-start(bf16[768,128]{1,0:T(8,128)(2,1)S(1)} %get-tuple-element.22), channel_id=1, source_target_pairs={{0,1},{1,2},{2,3},{3,4},{4,5},{5,6},{6,7},{7,0},{8,9},{9,10},{10,1... | collective-permute-start | bytes 589832 | tf_op jit(solution)/shard_map/ppermute | solution.py:234
  150.0 9.2 %collective-permute-start.11 = (bf16[768,128]{1,0:T(8,128)(2,1)S(1)}, bf16[768,128]{1,0:T(8,128)(2,1)S(1)}, u32[]{:S(2)}, u32[]{:S(2)}) collective-permute-start(bf16[768,128]{1,0:T(8,128)(2,1)S(1)} %get-tuple-element.23), channel_id=1, source_target_pairs={{1,0},{2,1},{3,2},{4,3},{5,4},{6,5},{7,6},{0,7},{9,8},{10,9},{11,1... | collective-permute-start | bytes 589832 | tf_op jit(solution)/shard_map/ppermute | solution.py:235
  159.4 8.3 %collective-permute-start.8 = (bf16[768,128]{1,0:T(8,128)(2,1)S(1)}, bf16[768,128]{1,0:T(8,128)(2,1)S(1)}, u32[]{:S(2)}, u32[]{:S(2)}) collective-permute-start(bf16[768,128]{1,0:T(8,128)(2,1)S(1)} %get-tuple-element.20), channel_id=1, source_target_pairs={{0,1},{1,2},{2,3},{3,4},{4,5},{5,6},{6,7},{7,0},{8,9},{9,10},{10,1... | collective-permute-start | bytes 589832 | tf_op jit(solution)/shard_map/ppermute | solution.py:234
  164.5 7.6 %collective-permute-start.12 = (bf16[768,128]{1,0:T(8,128)(2,1)S(1)}, bf16[768,128]{1,0:T(8,128)(2,1)S(1)}, u32[]{:S(2)}, u32[]{:S(2)}) collective-permute-start(bf16[768,128]{1,0:T(8,128)(2,1)S(1)} %get-tuple-element.21), channel_id=1, source_target_pairs={{1,0},{2,1},{3,2},{4,3},{5,4},{6,5},{7,6},{0,7},{9,8},{10,9},{11,1... | collective-permute-start | bytes 589832 | tf_op jit(solution)/shard_map/ppermute | solution.py:235
  173.5 1.0 copy-start.5
Sparse Core Ops, SparseCore 0:
  96.4 59.6 reduce-scatter.1

commit v5 on v3

--- a/solution.py
+++ b/solution.py
@@ -123,29 +123,18 @@
     out[...] = dot(hit.astype(jnp.bfloat16), returned[...], 1, 0).astype(jnp.bfloat16)
 
 
-def expert_kernel(
-    place, own, peer, gate_hbm, up_hbm, down_hbm, flat_hbm, backs,
-    rows, grads, gate, up, down, flat, sems, out_sems,
-):
-    def copies(rows_from, grads_from):
-        pairs = ((rows_from, rows), (gate_hbm, gate), (up_hbm, up), (grads_from, grads), (down_hbm, down))
-        return [pltpu.make_async_copy(a, b, sems.at[i]) for i, (a, b) in enumerate(pairs)]
-
+def expert_kernel(place, own, peer, gate, up, down, flat_hbm, backs, rows, grads, flat, out_sems):
     @pl.when(place[0] == 0)
     def _():
-        for copy in copies(own, peer):
-            copy.start()
+        rows[...] = own[...]
+        grads[...] = peer[...]
 
     @pl.when(place[0] != 0)
     def _():
-        for copy in copies(peer, own):
-            copy.start()
-
-    waits = copies(own, peer)
-    for copy in waits[:2]:
-        copy.wait()
+        rows[...] = peer[...]
+        grads[...] = own[...]
+
     gate_val = dot(rows[...], gate[...], 1, 0)
-    waits[2].wait()
     up_val = dot(rows[...], up[...], 1, 0)
     sigma = 1.0 / (1.0 + jnp.exp(-gate_val))
     activated = gate_val * sigma
@@ -157,8 +146,6 @@
     strip = units // replicas
     share = width // replicas
     per = share // 128
-    for copy in waits[3:]:
-        copy.wait()
     back_hid = dot(grads[...], down[...], 1, 1)
     for i in range(replicas):
         columns = slice(i * share, (i + 1) * share)
@@ -241,7 +228,7 @@
     down_by = [(j, i) for i, j in up_by]
     behind = lax.ppermute(packed, "expert", up_by)
     ahead = lax.ppermute(packed, "expert", down_by)
-    across = lax.ppermute(packed, "expert", [(i, (i + 32) % EXPERTS) for i in range(EXPERTS)])
+    across = lax.ppermute(behind, "expert", up_by)
     sent = pl.pallas_call(
         pick_kernel,
         out_shape=bf16((SLOTS, width)),
@@ -260,16 +247,12 @@
     flat, backs = pl.pallas_call(
         expert_kernel,
         out_shape=(bf16((replicas, 3 * units * share // 128, 128)), bf16((SLOTS, 2 * units))),
-        in_specs=[SMEM, HBM] + [ANY] * 4,
+        in_specs=[SMEM] + [VMEM] * 5,
         out_specs=(HBM, VMEM),
         scratch_shapes=[
             pltpu.VMEM((SLOTS, width), jnp.bfloat16),
             pltpu.VMEM((SLOTS, width), jnp.bfloat16),
-            pltpu.VMEM((width, units), jnp.bfloat16),
-            pltpu.VMEM((width, units), jnp.bfloat16),
-            pltpu.VMEM((units, width), jnp.bfloat16),
             pltpu.VMEM((replicas, 3 * units * share // 128, 128), jnp.bfloat16),
-            pltpu.SemaphoreType.DMA((5,)),
             pltpu.SemaphoreType.DMA((replicas,)),
         ],
         compiler_params=pltpu.CompilerParams(vmem_limit_bytes=48 * 1024 * 1024),

time: 171 us -> 171 us (level)
  waiting for transfers between devices: 30.8 us -> 27.2 us
  blocking collectives: 74.5 us -> 77.9 us
    ppermute x1, starting transfers between devices: 19.9 us -> 8.01 us  [shards(): across = lax.ppermute(behind, 'expert', up_by)]
    ppermute x1, waiting for transfers between devices: 11.1 us -> 0.01 us  [shards(): ahead = lax.ppermute(packed, 'expert', down_by)]
    all_to_all x1, blocking collectives: 30.9 us -> 38.3 us  [shards(): lax.all_to_all(sent.reshape(16, 4 * CAP, width), 'expert', split_axis=0,...]
    ppermute x1, starting transfers between devices: 1.92 us -> 9.2 us  [shards(): ahead = lax.ppermute(packed, 'expert', down_by)]
    ppermute x1, waiting for transfers between devices: 0.01 us -> 6.94 us  [shards(): across = lax.ppermute(behind, 'expert', up_by)]
    ppermute x1, starting transfers between devices: 7.27 us -> 11.5 us  [shards(): behind = lax.ppermute(packed, 'expert', up_by)]
    all_to_all x1, blocking collectives: 43.6 us -> 39.6 us  [shards(): lax.all_to_all(mine.astype(jnp.bfloat16).reshape(16, 4, CAP, half).transp...]
  transfers between devices with their start and end apart: 6 -> 6, of which waited for: 4 -> 5; matrix products, arithmetic and copies ran while one was open for 0% -> 0% of each run, Pallas kernels for 1% -> 1%
where the time goes in v5:
time: 171 us; the launch traced here: 170 us
  blocking collectives  77.9 us (46%)
  starting transfers between devices  34.8 us (20%)
  waiting for transfers between devices  27.2 us (16%)
  between operations  14.2 us (8%)
  Pallas kernels  13.3 us (8%)
  local copies, waits for them, and re-layouts  2.48 us (1%)
    all_to_all x1, blocking collectives, shards(): lax.all_to_all(mine.astype(jnp.bfloat16).reshape(16, 4, CAP, half).transp...  39.6 us
    all_to_all x1, blocking collectives, shards(): lax.all_to_all(sent.reshape(16, 4 * CAP, width), 'expert', split_axis=0,...  38.3 us
    reduce_scatter x1, waiting for transfers between devices, shards(): total = lax.psum_scatter(flat, 'dp', scatter_dimension=0, tiled=True)[0]  15.9 us
    ppermute x1, starting transfers between devices, shards(): behind = lax.ppermute(packed, 'expert', up_by)  11.5 us
    ppermute x1, starting transfers between devices, shards(): ahead = lax.ppermute(packed, 'expert', down_by)  9.2 us
    ppermute x1, starting transfers between devices, shards(): across = lax.ppermute(behind, 'expert', up_by)  8.01 us
    ppermute x1, waiting for transfers between devices, shards(): across = lax.ppermute(behind, 'expert', up_by)  6.94 us
    pallas_call x1, Pallas kernels, shards(): pl.pallas_call(expert_kernel, out_shape=(bf16((replicas, 3 * units * shar...  6.18 us
  transfers between devices with their start and end apart: 6, of which 5 were waited for; matrix products, arithmetic and copies ran while one was open for 0% of the time, Pallas kernels for 1%

profile of v5, /device:TPU:1, one launch (start us, length us, event | category | flops | bytes accessed | tf_op | source)
XLA Modules:
  0.0 170.1 jit_solution(12573953807383158741)
XLA Ops:
  7.2 0.0 reduce-scatter.2.cloned.1.call-start
  7.2 1.6 pack.1.own
  8.8 11.5 %collective-permute-start = (bf16[24,2176]{1,0:T(8,128)(2,1)}, bf16[24,2176]{1,0:T(8,128)(2,1)S(1)}, u32[]{:S(2)}, u32[]{:S(2)}) collective-permute-start(bf16[24,2176]{1,0:T(8,128)(2,1)} %pack.1.own), channel_id=1, source_target_pairs={{0,256},{16,272},{32,288},{48,304},{64,320},{80,336},{96,352},{112... | collective-permute-start | bytes 313352 | tf_op jit(solution)/shard_map/ppermute | solution.py:229
  20.3 9.2 %collective-permute-start.1 = (bf16[24,2176]{1,0:T(8,128)(2,1)}, bf16[24,2176]{1,0:T(8,128)(2,1)S(1)}, u32[]{:S(2)}, u32[]{:S(2)}) collective-permute-start(bf16[24,2176]{1,0:T(8,128)(2,1)} %pack.1.own), channel_id=1, source_target_pairs={{256,0},{272,16},{288,32},{304,48},{320,64},{336,80},{352,96},{368... | collective-permute-start | bytes 313352 | tf_op jit(solution)/shard_map/ppermute | solution.py:230
  29.5 0.6 collective-permute-done.behind
  30.1 8.0 %collective-permute-start.2 = (bf16[24,2176]{1,0:T(8,128)(2,1)S(1)}, bf16[24,2176]{1,0:T(8,128)(2,1)S(1)}, u32[]{:S(2)}, u32[]{:S(2)}) collective-permute-start(bf16[24,2176]{1,0:T(8,128)(2,1)S(1)} %collective-permute-done.behind), channel_id=1, source_target_pairs={{0,256},{16,272},{32,288},{48,304},{64,320},{80,336},{96,352},{112... | collective-permute-start | bytes 313352 | tf_op jit(solution)/shard_map/ppermute | solution.py:231
  38.2 0.1 pad_add_fusion.place
  38.2 0.0 collective-permute-done.1.ahead
  38.2 6.9 %collective-permute-done.2.across = bf16[24,2176]{1,0:T(8,128)(2,1)S(1)} collective-permute-done((bf16[24,2176]{1,0:T(8,128)(2,1)S(1)}, bf16[24,2176]{1,0:T(8,128)(2,1)S(1)}, u32[]{:S(2)}, u32[]{:S(2)}) %collective-permute-start.2) | collective-permute-done | bytes 104480 | tf_op jit(solution)/shard_map/ppermute | solution.py:231
  45.2 0.9 copy-done.3
  46.1 2.1 %pick.1 = bf16[256,2048]{1,0:T(8,128)(2,1)S(1)} custom-call(s32[2]{0:T(128)S(1)} %pad_add_fusion.place, bf16[24,2176]{1,0:T(8,128)(2,1)S(1)} %copy-done.3, bf16[24,2176]{1,0:T(8,128)(2,1)S(1)} %collective-permute-done.behind, bf16[24,2176]{1,0:T(8,128)(2,1)S(1)} %collective-permute-done.1.ahead, bf16[24,2176]{1,0:T(8,128)(2,1)S(1)} %collective-permute-done.2.across), custom_call_target="tpu_custom_call" | custom-call | tf_op jit(solution)/shard_map/pick/pallas_call | solution.py:232
  48.1 38.3 %all_to_all.10 = bf16[16,16,2048]{2,1,0:T(8,128)(2,1)S(1)} all-to-all(bf16[16,16,2048]{2,1,0:T(8,128)(2,1)S(1)} %bitcast.19), channel_id=1, replica_groups={{0,16,32,48,64,80,96,112,128,144,160,176,192,208,224,240},{256,272,288,..., dimensions={0} | all-to-all | bytes 2097152 | tf_op jit(solution)/shard_map/all_to_all | solution.py:241
  86.5 3.8 %collective-permute-start.3 = (bf16[256,2048]{1,0:T(8,128)(2,1)S(1)}, bf16[256,2048]{1,0:T(8,128)(2,1)S(1)}, u32[]{:S(2)}, u32[]{:S(2)}) collective-permute-start(bf16[256,2048]{1,0:T(8,128)(2,1)S(1)} %bitcast.20), channel_id=1, source_target_pairs={{0,8},{8,0},{1,9},{9,1},{2,10},{10,2},{3,11},{11,3},{4,12},{12,4},... | collective-permute-start | bytes 3145736 | tf_op jit(solution)/shard_map/ppermute | solution.py:245
  90.3 2.3 %collective-permute-done.3.peer = bf16[256,2048]{1,0:T(8,128)(2,1)S(1)} collective-permute-done((bf16[256,2048]{1,0:T(8,128)(2,1)S(1)}, bf16[256,2048]{1,0:T(8,128)(2,1)S(1)}, u32[]{:S(2)}, u32[]{:S(2)}) %collective-permute-start.3) | collective-permute-done | bytes 1048608 | tf_op jit(solution)/shard_map/ppermute | solution.py:245
  92.5 0.0 copy-done
  92.5 0.0 copy-done.1
  92.6 6.2 %expert.1 = (bf16[8,2304,128]{2,1,0:T(8,128)(2,1)}, bf16[256,768]{1,0:T(8,128)(2,1)S(1)}) custom-call(s32[1]{0:T(128)} %bitcast.1.cut.place, bf16[256,2048]{1,0:T(8,128)(2,1)S(1)} %bitcast.21, bf16[256,2048]{1,0:T(8,128)(2,1)S(1)} %collective-permute-done.3.peer, bf16[2048,384]{1,0:T(8,128)(2,1)S(1)} %bitcast.15, bf16[2048,384]{1,0:T(8,128)(2,1)S(1)} %bitcast.17, ...), custom_call_target="tpu_custom_call" | custom-call | tf_op jit(solution)/shard_map/expert/pallas_call | solution.py:247
  98.7 0.0 reduce-scatter.2.cloned.1.call-update
  98.8 1.3 rows.1
  100.1 2.3 %collective-permute-start.4 = (bf16[256,1024]{1,0:T(8,128)(2,1)S(1)}, bf16[256,1024]{1,0:T(8,128)(2,1)S(1)}, u32[]{:S(2)}, u32[]{:S(2)}) collective-permute-start(bf16[256,1024]{1,0:T(8,128)(2,1)S(1)} %get-tuple-element.13), channel_id=1, source_target_pairs={{0,8},{8,0},{1,9},{9,1},{2,10},{10,2},{3,11},{11,3},{4,12},{12,4},... | collective-permute-start | bytes 1572872 | tf_op jit(solution)/shard_map/ppermute | solution.py:271
  102.3 1.5 collective-permute-done.4
  103.9 0.1 add_convert_fusion
  104.0 0.2 reshape.29
  104.2 0.0 copy-start.4
  104.2 0.2 copy.11
  104.4 39.6 %all_to_all.11 = bf16[64,4,1024]{2,1,0:T(4,128)(2,1)S(1)} all-to-all(bf16[64,4,1024]{2,1,0:T(4,128)(2,1)S(1)} %bitcast.26), channel_id=1, replica_groups=mesh['expert'=64,'cuts'=2,'dp'=8] {'expert'}, dimensions={0} | all-to-all | bytes 1048576 | tf_op jit(solution)/shard_map/all_to_all | solution.py:272
  144.0 0.1 reshape.31.returned
  144.2 0.0 copy-done.4
  144.2 1.2 combine.1
  145.3 15.9 %reduce-scatter.2.cloned.1.call-done = bf16[1,2304,128]{2,1,0:T(8,128)(2,1)} async-done(((bf16[8,2304,128]{2,1,0:T(8,128)(2,1)}), bf16[1,2304,128]{2,1,0:T(8,128)(2,1)}) %reduce-scatter.2.cloned.1.call-update) | async-done | bytes 589840 | tf_op jit(solution)/shard_map/reduce_scatter | solution.py:261
  161.2 1.1 copy-done.2
  162.3 1.0 unpack.1
  (4 shorter events, 0.0 us)
Async XLA Ops:
  7.2 154.1 %reduce-scatter.2.cloned.1.call-start = ((), (), s32[]{:S(2)}) async-start(), calls=%async_computation.3 | async-start | bytes 5308416 | tf_op jit(solution)/shard_map/reduce_scatter | solution.py:261
  8.8 21.3 %collective-permute-start = (bf16[24,2176]{1,0:T(8,128)(2,1)}, bf16[24,2176]{1,0:T(8,128)(2,1)S(1)}, u32[]{:S(2)}, u32[]{:S(2)}) collective-permute-start(bf16[24,2176]{1,0:T(8,128)(2,1)} %pack.1.own), channel_id=1, source_target_pairs={{0,256},{16,272},{32,288},{48,304},{64,320},{80,336},{96,352},{112... | collective-permute-start | bytes 313352 | tf_op jit(solution)/shard_map/ppermute | solution.py:229
  20.3 17.9 %collective-permute-start.1 = (bf16[24,2176]{1,0:T(8,128)(2,1)}, bf16[24,2176]{1,0:T(8,128)(2,1)S(1)}, u32[]{:S(2)}, u32[]{:S(2)}) collective-permute-start(bf16[24,2176]{1,0:T(8,128)(2,1)} %pack.1.own), channel_id=1, source_target_pairs={{256,0},{272,16},{288,32},{304,48},{320,64},{336,80},{352,96},{368... | collective-permute-start | bytes 313352 | tf_op jit(solution)/shard_map/ppermute | solution.py:230
  30.1 15.0 %collective-permute-start.2 = (bf16[24,2176]{1,0:T(8,128)(2,1)S(1)}, bf16[24,2176]{1,0:T(8,128)(2,1)S(1)}, u32[]{:S(2)}, u32[]{:S(2)}) collective-permute-start(bf16[24,2176]{1,0:T(8,128)(2,1)S(1)} %collective-permute-done.behind), channel_id=1, source_target_pairs={{0,256},{16,272},{32,288},{48,304},{64,320},{80,336},{96,352},{112... | collective-permute-start | bytes 313352 | tf_op jit(solution)/shard_map/ppermute | solution.py:231
  38.2 54.3 %copy-start = (bf16[2048,1,384]{2,0,1:T(8,128)(2,1)S(1)}, bf16[2048,1,384]{2,0,1:T(8,128)(2,1)}, u32[]{:S(2)}) copy-start(bf16[2048,1,384]{2,0,1:T(8,128)(2,1)} %param.11) | copy-start | bytes 4718596
  38.2 54.3 %copy-start.1 = (bf16[2048,1,384]{2,0,1:T(8,128)(2,1)S(1)}, bf16[2048,1,384]{2,0,1:T(8,128)(2,1)}, u32[]{:S(2)}) copy-start(bf16[2048,1,384]{2,0,1:T(8,128)(2,1)} %param.12) | copy-start | bytes 4718596
  45.2 0.9 copy-start.3
  86.5 6.1 %collective-permute-start.3 = (bf16[256,2048]{1,0:T(8,128)(2,1)S(1)}, bf16[256,2048]{1,0:T(8,128)(2,1)S(1)}, u32[]{:S(2)}, u32[]{:S(2)}) collective-permute-start(bf16[256,2048]{1,0:T(8,128)(2,1)S(1)} %bitcast.20), channel_id=1, source_target_pairs={{0,8},{8,0},{1,9},{9,1},{2,10},{10,2},{3,11},{11,3},{4,12},{12,4},... | collective-permute-start | bytes 3145736 | tf_op jit(solution)/shard_map/ppermute | solution.py:245
  100.1 3.8 %collective-permute-start.4 = (bf16[256,1024]{1,0:T(8,128)(2,1)S(1)}, bf16[256,1024]{1,0:T(8,128)(2,1)S(1)}, u32[]{:S(2)}, u32[]{:S(2)}) collective-permute-start(bf16[256,1024]{1,0:T(8,128)(2,1)S(1)} %get-tuple-element.13), channel_id=1, source_target_pairs={{0,8},{8,0},{1,9},{9,1},{2,10},{10,2},{3,11},{11,3},{4,12},{12,4},... | collective-permute-start | bytes 1572872 | tf_op jit(solution)/shard_map/ppermute | solution.py:271
  104.2 39.9 %copy-start.4 = (s32[24,8]{0,1:T(8,128)S(1)}, s32[24,8]{0,1:T(8,128)}, u32[]{:S(2)}) copy-start(s32[24,8]{0,1:T(8,128)} %param.9) | copy-start | bytes 2308
  161.2 1.1 copy-start.2
Sparse Core Ops, SparseCore 0:
  98.9 62.2 reduce-scatter.1

commit v6 on v5

--- a/solution.py
+++ b/solution.py
@@ -123,7 +123,12 @@
     out[...] = dot(hit.astype(jnp.bfloat16), returned[...], 1, 0).astype(jnp.bfloat16)
 
 
-def expert_kernel(place, own, peer, gate, up, down, flat_hbm, backs, rows, grads, flat, out_sems):
+def expert_kernel(
+    place, own, peer, gate, up, down_hbm, flat_hbm, backs, rows, grads, down, flat, down_sem, out_sems
+):
+    load_down = pltpu.make_async_copy(down_hbm, down, down_sem)
+    load_down.start()
+
     @pl.when(place[0] == 0)
     def _():
         rows[...] = own[...]
@@ -146,7 +151,6 @@
     strip = units // replicas
     share = width // replicas
     per = share // 128
-    back_hid = dot(grads[...], down[...], 1, 1)
     for i in range(replicas):
         columns = slice(i * share, (i + 1) * share)
         part = dot(hidden_t, grads[:, columns], 1, 0).astype(jnp.bfloat16)
@@ -155,6 +159,8 @@
             start = 2 * per * units + (i * per + h) * strip
             for j in range(replicas):
                 flat[j, start : start + strip, :] = part[j * strip : (j + 1) * strip, lanes]
+    load_down.wait()
+    back_hid = dot(grads[...], down[...], 1, 1)
     both = jnp.concatenate((back_hid * up_val * slope, back_hid * activated), axis=1)
     backs[...] = both.astype(jnp.bfloat16)
     both_t = both.T.astype(jnp.bfloat16)
@@ -247,12 +253,14 @@
     flat, backs = pl.pallas_call(
         expert_kernel,
         out_shape=(bf16((replicas, 3 * units * share // 128, 128)), bf16((SLOTS, 2 * units))),
-        in_specs=[SMEM] + [VMEM] * 5,
+        in_specs=[SMEM] + [VMEM] * 4 + [ANY],
         out_specs=(HBM, VMEM),
         scratch_shapes=[
             pltpu.VMEM((SLOTS, width), jnp.bfloat16),
             pltpu.VMEM((SLOTS, width), jnp.bfloat16),
+            pltpu.VMEM((units, width), jnp.bfloat16),
             pltpu.VMEM((replicas, 3 * units * share // 128, 128), jnp.bfloat16),
+            pltpu.SemaphoreType.DMA,
             pltpu.SemaphoreType.DMA((replicas,)),
         ],
         compiler_params=pltpu.CompilerParams(vmem_limit_bytes=48 * 1024 * 1024),
@@ -288,7 +296,7 @@
         out_shape=(bf16((share, units)), bf16((share, units)), bf16((strip, width))),
         in_specs=[VMEM],
         out_specs=(VMEM,) * 3,
-        compiler_params=PARAMS,
+        compiler_params=pltpu.CompilerParams(vmem_limit_bytes=60 * 1024 * 1024),
         name="unpack",
     )(total)
     return (result, gate_grad[:, None, :], up_grad[:, None, :], down_grad[:, None, :])

time: 171 us -> 170 us (level)
  no operation moved by 1% of the time
where the time goes in v6:
time: 170 us; the launch traced here: 169 us
  blocking collectives  77.9 us (46%)
  starting transfers between devices  34.8 us (20%)
  waiting for transfers between devices  27.2 us (16%)
  between operations  14.2 us (8%)
  Pallas kernels  13.5 us (8%)
    all_to_all x1, blocking collectives, shards(): lax.all_to_all(mine.astype(jnp.bfloat16).reshape(16, 4, CAP, half).transp...  39.6 us
    all_to_all x1, blocking collectives, shards(): lax.all_to_all(sent.reshape(16, 4 * CAP, width), 'expert', split_axis=0,...  38.3 us
    reduce_scatter x1, waiting for transfers between devices, shards(): total = lax.psum_scatter(flat, 'dp', scatter_dimension=0, tiled=True)[0]  15.9 us
    ppermute x1, starting transfers between devices, shards(): behind = lax.ppermute(packed, 'expert', up_by)  11.5 us
    ppermute x1, starting transfers between devices, shards(): ahead = lax.ppermute(packed, 'expert', down_by)  9.2 us
    ppermute x1, starting transfers between devices, shards(): across = lax.ppermute(behind, 'expert', up_by)  8.01 us
    ppermute x1, waiting for transfers between devices, shards(): across = lax.ppermute(behind, 'expert', up_by)  6.94 us
    pallas_call x1, Pallas kernels, shards(): pl.pallas_call(expert_kernel, out_shape=(bf16((replicas, 3 * units * shar...  5.31 us
  transfers between devices with their start and end apart: 6, of which 5 were waited for; matrix products, arithmetic and copies ran while one was open for 0% of the time, Pallas kernels for 1%

profile of v6, /device:TPU:1, one launch (start us, length us, event | category | flops | bytes accessed | tf_op | source)
XLA Modules:
  0.0 169.2 jit_solution(11486600570167066029)
XLA Ops:
  7.2 0.0 reduce-scatter.2.cloned.1.call-start
  7.2 1.6 pack.1.own
  8.8 11.5 %collective-permute-start = (bf16[24,2176]{1,0:T(8,128)(2,1)}, bf16[24,2176]{1,0:T(8,128)(2,1)S(1)}, u32[]{:S(2)}, u32[]{:S(2)}) collective-permute-start(bf16[24,2176]{1,0:T(8,128)(2,1)} %pack.1.own), channel_id=1, source_target_pairs={{0,256},{16,272},{32,288},{48,304},{64,320},{80,336},{96,352},{112... | collective-permute-start | bytes 313352 | tf_op jit(solution)/shard_map/ppermute | solution.py:235
  20.3 9.2 %collective-permute-start.1 = (bf16[24,2176]{1,0:T(8,128)(2,1)}, bf16[24,2176]{1,0:T(8,128)(2,1)S(1)}, u32[]{:S(2)}, u32[]{:S(2)}) collective-permute-start(bf16[24,2176]{1,0:T(8,128)(2,1)} %pack.1.own), channel_id=1, source_target_pairs={{256,0},{272,16},{288,32},{304,48},{320,64},{336,80},{352,96},{368... | collective-permute-start | bytes 313352 | tf_op jit(solution)/shard_map/ppermute | solution.py:236
  29.5 0.6 collective-permute-done.behind
  30.1 8.0 %collective-permute-start.2 = (bf16[24,2176]{1,0:T(8,128)(2,1)S(1)}, bf16[24,2176]{1,0:T(8,128)(2,1)S(1)}, u32[]{:S(2)}, u32[]{:S(2)}) collective-permute-start(bf16[24,2176]{1,0:T(8,128)(2,1)S(1)} %collective-permute-done.behind), channel_id=1, source_target_pairs={{0,256},{16,272},{32,288},{48,304},{64,320},{80,336},{96,352},{112... | collective-permute-start | bytes 313352 | tf_op jit(solution)/shard_map/ppermute | solution.py:237
  38.2 0.1 pad_add_fusion.place
  38.2 0.0 copy-start
  38.2 0.0 collective-permute-done.1.ahead
  38.2 6.9 %collective-permute-done.2.across = bf16[24,2176]{1,0:T(8,128)(2,1)S(1)} collective-permute-done((bf16[24,2176]{1,0:T(8,128)(2,1)S(1)}, bf16[24,2176]{1,0:T(8,128)(2,1)S(1)}, u32[]{:S(2)}, u32[]{:S(2)}) %collective-permute-start.2) | collective-permute-done | bytes 104480 | tf_op jit(solution)/shard_map/ppermute | solution.py:237
  45.2 0.9 copy-done.2
  46.1 2.1 %pick.1 = bf16[256,2048]{1,0:T(8,128)(2,1)S(1)} custom-call(s32[2]{0:T(128)S(1)} %pad_add_fusion.place, bf16[24,2176]{1,0:T(8,128)(2,1)S(1)} %copy-done.2, bf16[24,2176]{1,0:T(8,128)(2,1)S(1)} %collective-permute-done.behind, bf16[24,2176]{1,0:T(8,128)(2,1)S(1)} %collective-permute-done.1.ahead, bf16[24,2176]{1,0:T(8,128)(2,1)S(1)} %collective-permute-done.2.across), custom_call_target="tpu_custom_call" | custom-call | tf_op jit(solution)/shard_map/pick/pallas_call | solution.py:238
  48.1 38.3 %all_to_all.10 = bf16[16,16,2048]{2,1,0:T(8,128)(2,1)S(1)} all-to-all(bf16[16,16,2048]{2,1,0:T(8,128)(2,1)S(1)} %bitcast.19), channel_id=1, replica_groups={{0,16,32,48,64,80,96,112,128,144,160,176,192,208,224,240},{256,272,288,..., dimensions={0} | all-to-all | bytes 2097152 | tf_op jit(solution)/shard_map/all_to_all | solution.py:247
  86.5 3.8 %collective-permute-start.3 = (bf16[256,2048]{1,0:T(8,128)(2,1)S(1)}, bf16[256,2048]{1,0:T(8,128)(2,1)S(1)}, u32[]{:S(2)}, u32[]{:S(2)}) collective-permute-start(bf16[256,2048]{1,0:T(8,128)(2,1)S(1)} %bitcast.20), channel_id=1, source_target_pairs={{0,8},{8,0},{1,9},{9,1},{2,10},{10,2},{3,11},{11,3},{4,12},{12,4},... | collective-permute-start | bytes 3145736 | tf_op jit(solution)/shard_map/ppermute | solution.py:251
  90.3 2.3 %collective-permute-done.3.peer = bf16[256,2048]{1,0:T(8,128)(2,1)S(1)} collective-permute-done((bf16[256,2048]{1,0:T(8,128)(2,1)S(1)}, bf16[256,2048]{1,0:T(8,128)(2,1)S(1)}, u32[]{:S(2)}, u32[]{:S(2)}) %collective-permute-start.3) | collective-permute-done | bytes 1048608 | tf_op jit(solution)/shard_map/ppermute | solution.py:251
  92.5 0.0 copy-done
  92.5 0.0 copy-done.1
  92.6 5.3 %expert.1 = (bf16[8,2304,128]{2,1,0:T(8,128)(2,1)}, bf16[256,768]{1,0:T(8,128)(2,1)S(1)}) custom-call(s32[1]{0:T(128)} %bitcast.1.cut.place, bf16[256,2048]{1,0:T(8,128)(2,1)S(1)} %bitcast.21, bf16[256,2048]{1,0:T(8,128)(2,1)S(1)} %collective-permute-done.3.peer, bf16[2048,384]{1,0:T(8,128)(2,1)S(1)} %bitcast.15, bf16[2048,384]{1,0:T(8,128)(2,1)S(1)} %bitcast.17, ...), custom_call_target="tpu_custom_call" | custom-call | tf_op jit(solution)/shard_map/expert/pallas_call | solution.py:253
  97.9 0.0 reduce-scatter.2.cloned.1.call-update
  97.9 1.3 rows.1
  99.2 2.3 %collective-permute-start.4 = (bf16[256,1024]{1,0:T(8,128)(2,1)S(1)}, bf16[256,1024]{1,0:T(8,128)(2,1)S(1)}, u32[]{:S(2)}, u32[]{:S(2)}) collective-permute-start(bf16[256,1024]{1,0:T(8,128)(2,1)S(1)} %get-tuple-element.13), channel_id=1, source_target_pairs={{0,8},{8,0},{1,9},{9,1},{2,10},{10,2},{3,11},{11,3},{4,12},{12,4},... | collective-permute-start | bytes 1572872 | tf_op jit(solution)/shard_map/ppermute | solution.py:279
  101.5 1.5 collective-permute-done.4
  103.0 0.1 add_convert_fusion
  103.1 0.2 reshape.29
  103.4 0.0 copy-start.3
  103.4 0.2 copy.11
  103.6 39.6 %all_to_all.11 = bf16[64,4,1024]{2,1,0:T(4,128)(2,1)S(1)} all-to-all(bf16[64,4,1024]{2,1,0:T(4,128)(2,1)S(1)} %bitcast.25), channel_id=1, replica_groups=mesh['expert'=64,'cuts'=2,'dp'=8] {'expert'}, dimensions={0} | all-to-all | bytes 1048576 | tf_op jit(solution)/shard_map/all_to_all | solution.py:280
  143.2 0.1 reshape.31.returned
  143.3 0.0 copy-done.3
  143.3 1.2 combine.1
  144.5 15.9 %reduce-scatter.2.cloned.1.call-done = bf16[1,2304,128]{2,1,0:T(8,128)(2,1)} async-done(((bf16[8,2304,128]{2,1,0:T(8,128)(2,1)}), bf16[1,2304,128]{2,1,0:T(8,128)(2,1)}) %reduce-scatter.2.cloned.1.call-update) | async-done | bytes 589840 | tf_op jit(solution)/shard_map/reduce_scatter | solution.py:269
  160.4 2.0 %unpack.1 = (bf16[256,384]{1,0:T(8,128)(2,1)}, bf16[256,384]{1,0:T(8,128)(2,1)}, bf16[48,2048]{1,0:T(8,128)(2,1)}) custom-call(bf16[2304,128]{1,0:T(8,128)(2,1)} %bitcast.27), custom_call_target="tpu_custom_call" | custom-call | tf_op jit(solution)/shard_map/unpack/pallas_call | solution.py:294
  (2 shorter events, 0.0 us)
Async XLA Ops:
  7.2 153.2 %reduce-scatter.2.cloned.1.call-start = ((), (), s32[]{:S(2)}) async-start(), calls=%async_computation.3 | async-start | bytes 5308416 | tf_op jit(solution)/shard_map/reduce_scatter | solution.py:269
  8.8 21.3 %collective-permute-start = (bf16[24,2176]{1,0:T(8,128)(2,1)}, bf16[24,2176]{1,0:T(8,128)(2,1)S(1)}, u32[]{:S(2)}, u32[]{:S(2)}) collective-permute-start(bf16[24,2176]{1,0:T(8,128)(2,1)} %pack.1.own), channel_id=1, source_target_pairs={{0,256},{16,272},{32,288},{48,304},{64,320},{80,336},{96,352},{112... | collective-permute-start | bytes 313352 | tf_op jit(solution)/shard_map/ppermute | solution.py:235
  20.3 17.9 %collective-permute-start.1 = (bf16[24,2176]{1,0:T(8,128)(2,1)}, bf16[24,2176]{1,0:T(8,128)(2,1)S(1)}, u32[]{:S(2)}, u32[]{:S(2)}) collective-permute-start(bf16[24,2176]{1,0:T(8,128)(2,1)} %pack.1.own), channel_id=1, source_target_pairs={{256,0},{272,16},{288,32},{304,48},{320,64},{336,80},{352,96},{368... | collective-permute-start | bytes 313352 | tf_op jit(solution)/shard_map/ppermute | solution.py:236
  30.1 15.0 %collective-permute-start.2 = (bf16[24,2176]{1,0:T(8,128)(2,1)S(1)}, bf16[24,2176]{1,0:T(8,128)(2,1)S(1)}, u32[]{:S(2)}, u32[]{:S(2)}) collective-permute-start(bf16[24,2176]{1,0:T(8,128)(2,1)S(1)} %collective-permute-done.behind), channel_id=1, source_target_pairs={{0,256},{16,272},{32,288},{48,304},{64,320},{80,336},{96,352},{112... | collective-permute-start | bytes 313352 | tf_op jit(solution)/shard_map/ppermute | solution.py:237
  38.2 54.3 %copy-start = (bf16[2048,1,384]{2,0,1:T(8,128)(2,1)S(1)}, bf16[2048,1,384]{2,0,1:T(8,128)(2,1)}, u32[]{:S(2)}) copy-start(bf16[2048,1,384]{2,0,1:T(8,128)(2,1)} %param.11) | copy-start | bytes 4718596
  38.2 54.3 %copy-start.1 = (bf16[2048,1,384]{2,0,1:T(8,128)(2,1)S(1)}, bf16[2048,1,384]{2,0,1:T(8,128)(2,1)}, u32[]{:S(2)}) copy-start(bf16[2048,1,384]{2,0,1:T(8,128)(2,1)} %param.12) | copy-start | bytes 4718596
  45.2 0.9 copy-start.2
  86.5 6.1 %collective-permute-start.3 = (bf16[256,2048]{1,0:T(8,128)(2,1)S(1)}, bf16[256,2048]{1,0:T(8,128)(2,1)S(1)}, u32[]{:S(2)}, u32[]{:S(2)}) collective-permute-start(bf16[256,2048]{1,0:T(8,128)(2,1)S(1)} %bitcast.20), channel_id=1, source_target_pairs={{0,8},{8,0},{1,9},{9,1},{2,10},{10,2},{3,11},{11,3},{4,12},{12,4},... | collective-permute-start | bytes 3145736 | tf_op jit(solution)/shard_map/ppermute | solution.py:251
  99.2 3.8 %collective-permute-start.4 = (bf16[256,1024]{1,0:T(8,128)(2,1)S(1)}, bf16[256,1024]{1,0:T(8,128)(2,1)S(1)}, u32[]{:S(2)}, u32[]{:S(2)}) collective-permute-start(bf16[256,1024]{1,0:T(8,128)(2,1)S(1)} %get-tuple-element.13), channel_id=1, source_target_pairs={{0,8},{8,0},{1,9},{9,1},{2,10},{10,2},{3,11},{11,3},{4,12},{12,4},... | collective-permute-start | bytes 1572872 | tf_op jit(solution)/shard_map/ppermute | solution.py:279
  103.4 39.9 %copy-start.3 = (s32[24,8]{0,1:T(8,128)S(1)}, s32[24,8]{0,1:T(8,128)}, u32[]{:S(2)}) copy-start(s32[24,8]{0,1:T(8,128)} %param.9) | copy-start | bytes 2308
Sparse Core Ops, SparseCore 0:
  98.0 62.2 reduce-scatter.1
